TPU v7x, 32 devices: a whole 2x2x4 slice. The times are simulated.
32 devices in a mesh: ctx: 8 (over z, y), tp: 4 (over x, core).
Axes of the slice: x: 2, y: 2, z: 4, core: 2. Of those that a mesh axis runs over, the one named last changes fastest.
Arguments:
- tokens: bfloat16 [2048, 2048], P('ctx'), may hold values from -6 to 6
- w_query: bfloat16 [2048, 4096], P(None, 'tp'), may hold values from -0.125 to 0.125
- w_key: bfloat16 [2048, 512], replicated, may hold values from -0.125 to 0.125
- w_value: bfloat16 [2048, 512], replicated, may hold values from -0.125 to 0.125
- w_out: bfloat16 [4096, 2048], P('tp'), may hold values from -0.09375 to 0.09375
- query_gain: float32 [128], replicated, may hold values from 0.5 to 2
- key_gain: float32 [128], replicated, may hold values from 0.5 to 2
- doc_lengths: int32 [16], replicated, may hold values from 1 to 1024, as said below
Outputs:
- layer_out: bfloat16 [2048, 2048], P('ctx', 'tp')
Inputs may be any that keep to these rules, and one draw needn't show every extreme that they name: `doc_lengths`: the lengths sum to 2048; the second-to-last document has exactly 1024 tokens and the last one exactly 128.
All inputs are finite; a program needn't handle non-finite values.
Results may differ from a plain program's by a relative error of at most 0.014.
Values may be sent and summed in bfloat16 or wider, within the bound.
A program may use at most 64 MiB of HBM per device.

v0:
```python
import jax
import jax.numpy as jnp
from jax import lax
from jax.sharding import PartitionSpec as P

H = 32
KVH = 4
HD = 128


EPSILON = 1e-06
ROPE_BASE = 1000000.0
NEGATIVE = -1e30


def passed_along(block, axis, distance):
    devices = range(lax.axis_size(axis))
    route = [(i - distance, i) for i in devices if i - distance in devices]
    return lax.ppermute(block, axis, route)


def doc_starts(positions, doc_lengths):
    doc_ends = jnp.cumsum(doc_lengths)
    before = doc_ends[None, :] <= positions[:, None]
    return jnp.sum(jnp.where(before, doc_lengths[None, :], 0), axis=1)


def norm_rotate(inputs, gain_vec, offsets):
    full_width = inputs.shape[-1]
    half_width = full_width // 2
    inv_norm = lax.rsqrt(jnp.mean(inputs * inputs, axis=-1, keepdims=True) + EPSILON)
    normed = inputs * inv_norm * gain_vec
    frequency = ROPE_BASE ** (-2.0 * jnp.arange(half_width, dtype=jnp.float32) / full_width)
    angles = offsets[:, None] * frequency[None, :]
    cosine = jnp.cos(angles)[:, None, :]
    sine_part = jnp.sin(angles)[:, None, :]
    first_half = normed[..., :half_width]
    second_half = normed[..., half_width:]
    return jnp.concatenate(
        [
            first_half * cosine - second_half * sine_part,
            second_half * cosine + first_half * sine_part,
        ],
        axis=-1,
    )


def local(tokens, w_query, w_key, w_value, w_out, query_gain, key_gain, doc_lengths):
    row_count = tokens.shape[0]
    head_count = w_query.shape[1] // HD
    tp_rank = lax.axis_index("tp")
    my_block = lax.axis_index("ctx")
    reach_blocks = min(16, lax.axis_size("ctx") // 2)
    kv_head = tp_rank * head_count // (H // KVH)
    key_cols = lax.dynamic_slice_in_dim(w_key, kv_head * HD, HD, 1)
    value_cols = lax.dynamic_slice_in_dim(w_value, kv_head * HD, HD, 1)
    positions = my_block * row_count + jnp.arange(row_count, dtype=jnp.int32)
    starts_local = doc_starts(positions, doc_lengths)
    offsets = (positions - starts_local).astype(jnp.float32)
    query_proj = jnp.dot(tokens, w_query, preferred_element_type=jnp.float32).reshape(
        row_count, head_count, HD
    )
    queries = (
        norm_rotate(query_proj, query_gain, offsets)
        .astype(jnp.bfloat16)
        .reshape(row_count * head_count, HD)
    )
    key_proj = jnp.dot(tokens, key_cols, preferred_element_type=jnp.float32).reshape(
        row_count, 1, HD
    )
    keys_local = (
        norm_rotate(key_proj, key_gain, offsets).reshape(row_count, HD).astype(jnp.bfloat16)
    )
    values_local = jnp.dot(tokens, value_cols, preferred_element_type=jnp.float32).astype(
        jnp.bfloat16
    )
    key_value = jnp.stack([keys_local, values_local])
    query_pos = jnp.repeat(positions, head_count)
    query_start = jnp.repeat(starts_local, head_count)

    def attend(softmax_state, kv_block, key_block):
        row_peak, row_total, weighted = softmax_state
        key_pos = key_block * row_count + jnp.arange(row_count, dtype=jnp.int32)
        scores = lax.dot_general(
            queries, kv_block[0], (((1,), (1,)), ((), ())), preferred_element_type=jnp.float32
        ) * HD ** (-0.5)
        visible = (key_pos[None, :] <= query_pos[:, None]) & (
            key_pos[None, :] >= query_start[:, None]
        )
        new_peak = jnp.maximum(row_peak, jnp.max(jnp.where(visible, scores, NEGATIVE), axis=1))
        weights = jnp.where(visible, jnp.exp(scores - new_peak[:, None]), 0.0)
        factor = jnp.exp(row_peak - new_peak)
        row_total = row_total * factor + jnp.sum(weights, axis=1)
        weighted = weighted * factor[:, None] + jnp.dot(
            weights.astype(jnp.bfloat16), kv_block[1], preferred_element_type=jnp.float32
        )
        return (new_peak, row_total, weighted)

    def use_tile(softmax_state, kv_block, key_block):
        return attend(softmax_state, kv_block, key_block)

    query_rows = row_count * head_count
    initial = (
        jnp.full((query_rows,), NEGATIVE, jnp.float32),
        jnp.zeros((query_rows,), jnp.float32),
        jnp.zeros((query_rows, HD), jnp.float32),
    )
    softmax_state = attend(initial, key_value, my_block)
    levels = reach_blocks.bit_length() - 1
    window = key_value[None]
    for level in range(levels):
        arrived = passed_along(window, "ctx", 2**level)
        window = jnp.concatenate([arrived, window], axis=0)
    far_block = passed_along(key_value, "ctx", reach_blocks)
    softmax_state = use_tile(softmax_state, far_block, my_block - reach_blocks)
    window_count = 2**levels

    def visit(index, state_in):
        return use_tile(state_in, window[index], my_block - (window_count - 1) + index)

    softmax_state = lax.fori_loop(0, window_count - 1, visit, softmax_state)
    attended = (
        (softmax_state[2] / softmax_state[1][:, None])
        .astype(jnp.bfloat16)
        .reshape(row_count, head_count * HD)
    )
    head_term = jnp.dot(attended, w_out, preferred_element_type=jnp.float32)
    return lax.psum_scatter(head_term.astype(jnp.bfloat16), "tp", scatter_dimension=1, tiled=True)


def solution(mesh):
    return jax.shard_map(
        local,
        mesh=mesh,
        in_specs=(P("ctx", None), P(None, "tp"), P(), P(), P("tp", None), P(), P(), P()),
        out_specs=P("ctx", "tp"),
        check_vma=False,
    )
```

profile of v0, /device:TPU:0, one launch (start us, length us, event | category | flops | bytes accessed | tf_op | source)
XLA Modules:
  0.0 110.3 jit_solution(16585666365179853985)
XLA Ops:
  6.6 1.5 %copy-done = bf16[2048,512]{1,0:T(8,128)(2,1)S(1)} copy-done((bf16[2048,512]{1,0:T(8,128)(2,1)S(1)}, bf16[2048,512]{1,0:T(8,128)(2,1)}, u32[]{:S(2)}) %copy-start) | copy-done | bytes 2097176
  8.1 1.7 %multiply_reduce_fusion.1 = (f32[256]{0:T(256)S(1)}, f32[128,256]{1,0:T(8,128)S(1)}) fusion(bf16[256,2048]{1,0:T(8,128)(2,1)} %param.10, bf16[2048,512]{1,0:T(8,128)(2,1)S(1)} %copy-done, s32[]{:T(128)S(6)} %select_n.53), kind=kOutput, calls=%fused_computation.69 | convolution fusion | flops 134283008 | bytes 1704964 | tf_op jit(solution)/shard_map/dot_general | solution.py:68
  10.8 0.7 select_reduce_fusion.3
  11.5 1.5 %convolution_convert_fusion.1 = bf16[128,256]{1,0:T(8,128)(2,1)S(1)} fusion(bf16[256,2048]{1,0:T(8,128)(2,1)S(1)} %copy-done.2, bf16[2048,512]{1,0:T(8,128)(2,1)} %param.13, s32[]{:T(128)S(6)} %select_n.53), kind=kOutput, calls=%fused_computation.40 | convolution fusion | flops 134250496 | bytes 1638404 | tf_op jit(solution)/shard_map/dot_general | solution.py:74
  14.2 6.6 %collective-permute-start = (bf16[2,256,128]{1,2,0:T(8,128)(2,1)}, bf16[2,256,128]{1,2,0:T(8,128)(2,1)}, u32[]{:S(2)}, u32[]{:S(2)}) collective-permute-start(bf16[2,256,128]{1,2,0:T(8,128)(2,1)} %get-tuple-element.320), channel_id=1, source_target_pairs={{0,16},{4,20},{8,24},{12,28},{1,17},{5,21},{9,25},{13,29},{2,18},{... | collective-permute-start | bytes 393224 | tf_op jit(solution)/shard_map/ppermute | solution.py:19
  20.8 4.1 %collective-permute-start.1 = (bf16[1,2,256,128]{2,3,1,0:T(8,128)(2,1)S(1)}, bf16[1,2,256,128]{2,3,1,0:T(8,128)(2,1)}, u32[]{:S(2)}, u32[]{:S(2)}) collective-permute-start(bf16[1,2,256,128]{2,3,1,0:T(8,128)(2,1)S(1)} %get-tuple-element.319), channel_id=1, source_target_pairs={{0,4},{4,8},{8,12},{12,16},{16,20},{20,24},{24,28},{1,5},{5,9},{9,... | collective-permute-start | bytes 393224 | tf_op jit(solution)/shard_map/ppermute | solution.py:19
  24.8 1.2 %multiply_cosine_fusion = (f32[256,64]{1,0:T(8,128)}, f32[256,64]{1,0:T(8,128)}) fusion(f32[64]{0:T(128)S(1)} %multiply_power_fusion, f32[256]{0:T(256)S(1)} %subtract_convert_fusion.1), kind=kLoop, calls=%fused_computation.65 | loop fusion | flops 16384 | bytes 132352 | tf_op jit(solution)/shard_map/cos | solution.py:35
  26.1 3.4 %convolution_bitcast_fusion = f32[32,8,8,128]{3,1,2,0:T(8,128)S(1)} fusion(bf16[256,2048]{1,0:T(8,128)(2,1)S(1)} %copy-done.2, bf16[2048,1024]{1,0:T(8,128)(2,1)} %param.11), kind=kOutput, calls=%fused_computation.35 | convolution fusion | flops 1073741824 | bytes 6291456 | tf_op jit(solution)/shard_map/dot_general | solution.py:60
  31.3 1.0 multiply_multiply_fusion
  33.2 2.0 %select_reduce_fusion.2 = (f32[2048]{0:T(1024)S(1)}, f32[2048,256]{0,1:T(8,128)}) fusion(s32[2048]{0:T(1024)S(1)} %ge.55, s32[2048]{0:T(1024)S(1)} %copy-done.14, s32[256]{0:T(256)S(1)} %iota_add_fusion.2, bf16[2048,128]{1,0:T(8,128)(2,1)S(1)} %pad_maximum_fusion, bf16[256,1,64]{0,2,1:T(8,128)(2,1)S(1)} %copy-done.13, bf16[256,1,64]{0,2,1:T(8,128)(2,1)S(1)} %copy-done.11), kind=kOutput, calls=%fused_computation.32 | convolution fusion | flops 137492480 | bytes 2712576 | tf_op jit(solution)/shard_map/dot_general | solution.py:84
  35.2 2.9 %fusion.18 = (f32[2048]{0:T(1024)S(1)}, f32[2048]{0:T(1024)S(1)}, f32[2048,256]{0,1:T(8,128)S(1)}) fusion(f32[2048,256]{0,1:T(8,128)} %get-tuple-element.328, f32[2048]{0:T(1024)S(1)} %broadcast_maximum_fusion, s32[2048]{0:T(1024)S(1)} %ge.55, s32[2048]{0:T(1024)S(1)} %copy-done.14, s32[256]{0:T(256)S(1)} %iota_add_fusion.2, s32[256]{0:T(256)S(1)} %iota_add_fusion.1, ...), kind=kOutput, calls=%fused_computation.37 | convolution fusion | flops 140505088 | bytes 4827136 | tf_op jit(solution)/shard_map/dot_general | solution.py:84
  38.2 1.1 pad_maximum_fusion.2
  39.2 3.1 %collective-permute-start.2 = (bf16[2,2,256,128]{2,3,1,0:T(8,128)(2,1)S(1)}, bf16[2,2,256,128]{2,3,1,0:T(8,128)(2,1)S(1)}, u32[]{:S(2)}, u32[]{:S(2)}) collective-permute-start(bf16[2,2,256,128]{2,3,1,0:T(8,128)(2,1)S(1)} %pad_maximum_fusion.2), channel_id=1, source_target_pairs={{0,8},{4,12},{8,16},{12,20},{16,24},{20,28},{1,9},{5,13},{9,17},{1... | collective-permute-start | bytes 786440 | tf_op jit(solution)/shard_map/ppermute | solution.py:19
  43.0 1.2 %fusion.16 = f32[2048,128]{1,0:T(8,128)S(1)} fusion(bf16[128,256]{1,0:T(8,128)(2,1)S(1)} %copy-done.9, f32[2048,256]{0,1:T(8,128)S(1)} %copy-done.16, f32[2048]{0:T(1024)S(1)} %broadcast_maximum_fusion, s32[2048]{0:T(1024)S(1)} %ge.55, s32[2048]{0:T(1024)S(1)} %copy-done.14, s32[256]{0:T(256)S(1)} %iota_add_fusion.2, f32[2048]{0:T(1024)S(1)} %get-tuple-element.312, ...), kind=kOutput, calls=%fused_computation.28 | convolution fusion | flops 137887744 | bytes 3253248 | tf_op jit(solution)/shard_map/dot_general | solution.py:94
  44.1 2.7 %convolution_add_fusion.1 = f32[2048,128]{1,0:T(8,128)} fusion(f32[2048,128]{1,0:T(8,128)S(1)} %fusion.16, f32[2048,256]{0,1:T(8,128)S(1)} %get-tuple-element.329, f32[2048]{0:T(1024)S(1)} %get-tuple-element.394, s32[2048]{0:T(1024)S(1)} %ge.55, s32[2048]{0:T(1024)S(1)} %copy-done.14, s32[256]{0:T(256)S(1)} %iota_add_fusion.1, ...), kind=kOutput, calls=%fused_computation.26 | convolution fusion | flops 137625600 | bytes 4285440 | tf_op jit(solution)/shard_map/dot_general | solution.py:94
  47.1 1.8 %pad_maximum_fusion.1 = bf16[4,2,256,128]{2,3,1,0:T(8,128)(2,1)} fusion(bf16[1,2,256,128]{2,3,1,0:T(8,128)(2,1)S(1)} %get-tuple-element.319, bf16[1,2,256,128]{2,3,1,0:T(8,128)(2,1)} %collective-permute-done.1, bf16[2,2,256,128]{2,3,1,0:T(8,128)(2,1)S(1)} %collective-permute-done.2), kind=kLoop, calls=%fused_computation.59 | loop fusion | flops 524288 | bytes 1048576 | tf_op jit(solution)/shard_map/concatenate | solution.py:113
  48.9 24.1 %while.20 = (s32[]{:T(128)}, f32[2048]{0:T(1024)S(1)}, f32[2048]{0:T(1024)S(1)}, f32[2048,128]{1,0:T(8,128)}, s32[]{:T(128)}, /*index=5*/bf16[4,2,256,128]{2,3,1...) while((s32[]{:T(128)}, f32[2048]{0:T(1024)S(1)}, ...), condition=%wide.region_11.12_spmd.clone, body=%wide.region_8.11_spmd.clone.sunk | while | flops 278401280 | bytes 26057980 | solution.py:121
  49.3 1.9 %select_reduce_fusion.5 = (f32[2048]{0:T(1024)S(1)}, f32[2048,256]{0,1:T(8,128)S(1)}) fusion(s32[2048]{0:T(1024)S(1)} %ge.123, s32[2048]{0:T(1024)S(1)} %le.188, s32[256]{0:T(256)S(1)} %iota_add_fusion.4, bf16[2048,128]{1,0:T(8,128)(2,1)} %get-tuple-element.425, bf16[4,2,256,128]{2,3,1,0:T(8,128)(2,1)} %get-tuple-element.424, s32[]{:T(128)} %get-tuple-element.406), kind=kOutput, calls=%fused_computation.6.clone.1 | convolution fusion | flops 137361408 | bytes 2713088 | tf_op jit(solution)/shard_map/while/body/eval_jaxpr/dot_general | solution.py:84
  51.2 1.3 %copy-done.1 = f32[2048,256]{0,1:T(8,128)} copy-done((f32[2048,256]{0,1:T(8,128)}, f32[2048,256]{0,1:T(8,128)S(1)}, u32[]{:S(2)}) %copy-start.1) | copy-done | bytes 2097176 | tf_op jit(solution)/shard_map/while
  53.2 2.7 %convolution_add_fusion.4 = f32[2048,128]{1,0:T(8,128)S(1)} fusion(f32[2048,256]{0,1:T(8,128)} %copy-done.1, f32[2048,128]{1,0:T(8,128)S(1)} %copy-done.3, f32[2048]{0:T(1024)S(1)} %max.26, s32[2048]{0:T(1024)S(1)} %ge.123, s32[2048]{0:T(1024)S(1)} %le.188, s32[256]{0:T(256)S(1)} %iota_add_fusion.4, f32[2048]{0:T(1024)S(1)} %get-tuple-element.392, ...), kind=kOutput, calls=%fused_computation.4.clone.1 | convolution fusion | flops 137887744 | bytes 4294148 | tf_op jit(solution)/shard_map/while/body/eval_jaxpr/dot_general | solution.py:94
  56.0 1.0 copy-done.4
  57.3 1.9 %select_reduce_fusion.5 = (f32[2048]{0:T(1024)S(1)}, f32[2048,256]{0,1:T(8,128)S(1)}) fusion(s32[2048]{0:T(1024)S(1)} %ge.123, s32[2048]{0:T(1024)S(1)} %le.188, s32[256]{0:T(256)S(1)} %iota_add_fusion.4, bf16[2048,128]{1,0:T(8,128)(2,1)} %get-tuple-element.425, bf16[4,2,256,128]{2,3,1,0:T(8,128)(2,1)} %get-tuple-element.424, s32[]{:T(128)} %get-tuple-element.406), kind=kOutput, calls=%fused_computation.6.clone.1 | convolution fusion | flops 137361408 | bytes 2713088 | tf_op jit(solution)/shard_map/while/body/eval_jaxpr/dot_general | solution.py:84
  59.3 1.3 %copy-done.1 = f32[2048,256]{0,1:T(8,128)} copy-done((f32[2048,256]{0,1:T(8,128)}, f32[2048,256]{0,1:T(8,128)S(1)}, u32[]{:S(2)}) %copy-start.1) | copy-done | bytes 2097176 | tf_op jit(solution)/shard_map/while
  61.2 2.7 %convolution_add_fusion.4 = f32[2048,128]{1,0:T(8,128)S(1)} fusion(f32[2048,256]{0,1:T(8,128)} %copy-done.1, f32[2048,128]{1,0:T(8,128)S(1)} %copy-done.3, f32[2048]{0:T(1024)S(1)} %max.26, s32[2048]{0:T(1024)S(1)} %ge.123, s32[2048]{0:T(1024)S(1)} %le.188, s32[256]{0:T(256)S(1)} %iota_add_fusion.4, f32[2048]{0:T(1024)S(1)} %get-tuple-element.392, ...), kind=kOutput, calls=%fused_computation.4.clone.1 | convolution fusion | flops 137887744 | bytes 4294148 | tf_op jit(solution)/shard_map/while/body/eval_jaxpr/dot_general | solution.py:94
  64.0 1.0 copy-done.4
  65.4 1.9 %select_reduce_fusion.5 = (f32[2048]{0:T(1024)S(1)}, f32[2048,256]{0,1:T(8,128)S(1)}) fusion(s32[2048]{0:T(1024)S(1)} %ge.123, s32[2048]{0:T(1024)S(1)} %le.188, s32[256]{0:T(256)S(1)} %iota_add_fusion.4, bf16[2048,128]{1,0:T(8,128)(2,1)} %get-tuple-element.425, bf16[4,2,256,128]{2,3,1,0:T(8,128)(2,1)} %get-tuple-element.424, s32[]{:T(128)} %get-tuple-element.406), kind=kOutput, calls=%fused_computation.6.clone.1 | convolution fusion | flops 137361408 | bytes 2713088 | tf_op jit(solution)/shard_map/while/body/eval_jaxpr/dot_general | solution.py:84
  67.3 1.3 %copy-done.1 = f32[2048,256]{0,1:T(8,128)} copy-done((f32[2048,256]{0,1:T(8,128)}, f32[2048,256]{0,1:T(8,128)S(1)}, u32[]{:S(2)}) %copy-start.1) | copy-done | bytes 2097176 | tf_op jit(solution)/shard_map/while
  69.2 2.7 %convolution_add_fusion.4 = f32[2048,128]{1,0:T(8,128)S(1)} fusion(f32[2048,256]{0,1:T(8,128)} %copy-done.1, f32[2048,128]{1,0:T(8,128)S(1)} %copy-done.3, f32[2048]{0:T(1024)S(1)} %max.26, s32[2048]{0:T(1024)S(1)} %ge.123, s32[2048]{0:T(1024)S(1)} %le.188, s32[256]{0:T(256)S(1)} %iota_add_fusion.4, f32[2048]{0:T(1024)S(1)} %get-tuple-element.392, ...), kind=kOutput, calls=%fused_computation.4.clone.1 | convolution fusion | flops 137887744 | bytes 4294148 | tf_op jit(solution)/shard_map/while/body/eval_jaxpr/dot_general | solution.py:94
  72.0 1.0 copy-done.4
  73.0 1.6 %divide_convert_fusion = bf16[2048,128]{1,0:T(8,128)(2,1)S(1)} fusion(f32[2048,128]{1,0:T(8,128)} %get-tuple-element.219, f32[2048]{0:T(1024)S(1)} %get-tuple-element.220), kind=kLoop, calls=%fused_computation.41 | loop fusion | flops 524288 | bytes 1581056 | tf_op jit(solution)/shard_map/convert_element_type | solution.py:124
  74.8 4.4 %convolution_convert_fusion = bf16[256,2048]{1,0:T(8,128)(2,1)} fusion(bf16[256,1024]{1,0:T(8,128)(2,1)S(1)} %reshape.230, bf16[1024,2048]{1,0:T(8,128)(2,1)} %param.14), kind=kOutput, calls=%fused_computation.25 | convolution fusion | flops 1074266112 | bytes 5767168 | tf_op jit(solution)/shard_map/dot_general | solution.py:127
  79.2 24.2 %reduce-scatter.2.cloned.1.call-done = bf16[256,512]{1,0:T(8,128)(2,1)} async-done(((bf16[256,2048]{1,0:T(8,128)(2,1)}), bf16[256,512]{1,0:T(8,128)(2,1)}) %reduce-scatter.2.cloned.1.call-update) | async-done | bytes 262160 | tf_op jit(solution)/shard_map/reduce_scatter | solution.py:128
  (99 shorter events, 8.8 us)
Async XLA Ops:
  6.5 1.6 %copy-start = (bf16[2048,512]{1,0:T(8,128)(2,1)S(1)}, bf16[2048,512]{1,0:T(8,128)(2,1)}, u32[]{:S(2)}) copy-start(bf16[2048,512]{1,0:T(8,128)(2,1)} %param.12) | copy-start | bytes 6291460
  6.5 5.0 %copy-start.2 = (bf16[256,2048]{1,0:T(8,128)(2,1)S(1)}, bf16[256,2048]{1,0:T(8,128)(2,1)}, u32[]{:S(2)}) copy-start(bf16[256,2048]{1,0:T(8,128)(2,1)} %param.10) | copy-start | bytes 3145732
  6.5 6.5 %copy-start.15 = (f32[128]{0:T(128)S(1)}, f32[128]{0:T(128)}, u32[]{:S(2)}) copy-start(f32[128]{0:T(128)} %param.16) | copy-start | bytes 1540
  6.5 96.9 %reduce-scatter.2.cloned.1.call-start = ((), (), s32[]{:S(2)}) async-start(), calls=%async_computation.1 | async-start | bytes 1310720 | tf_op jit(solution)/shard_map/reduce_scatter | solution.py:128
  13.1 11.8 %copy-start.8 = (bf16[128,256]{1,0:T(8,128)(2,1)}, bf16[128,256]{1,0:T(8,128)(2,1)S(1)}, u32[]{:S(2)}) copy-start(bf16[128,256]{1,0:T(8,128)(2,1)S(1)} %convolution_convert_fusion.1) | copy-start | bytes 196612
  13.5 11.3 %copy-start.10 = (bf16[256,1,64]{0,2,1:T(8,128)(2,1)}, bf16[256,1,64]{0,2,1:T(8,128)(2,1)S(1)}, u32[]{:S(2)}) copy-start(bf16[256,1,64]{0,2,1:T(8,128)(2,1)S(1)} %get-tuple-element.317) | copy-start | bytes 98308
  13.5 11.3 %copy-start.12 = (bf16[256,1,64]{0,2,1:T(8,128)(2,1)}, bf16[256,1,64]{0,2,1:T(8,128)(2,1)S(1)}, u32[]{:S(2)}) copy-start(bf16[256,1,64]{0,2,1:T(8,128)(2,1)S(1)} %get-tuple-element.318) | copy-start | bytes 98308
  14.2 21.0 %collective-permute-start = (bf16[2,256,128]{1,2,0:T(8,128)(2,1)}, bf16[2,256,128]{1,2,0:T(8,128)(2,1)}, u32[]{:S(2)}, u32[]{:S(2)}) collective-permute-start(bf16[2,256,128]{1,2,0:T(8,128)(2,1)} %get-tuple-element.320), channel_id=1, source_target_pairs={{0,16},{4,20},{8,24},{12,28},{1,17},{5,21},{9,25},{13,29},{2,18},{... | collective-permute-start | bytes 393224 | tf_op jit(solution)/shard_map/ppermute | solution.py:19
  20.8 17.4 %collective-permute-start.1 = (bf16[1,2,256,128]{2,3,1,0:T(8,128)(2,1)S(1)}, bf16[1,2,256,128]{2,3,1,0:T(8,128)(2,1)}, u32[]{:S(2)}, u32[]{:S(2)}) collective-permute-start(bf16[1,2,256,128]{2,3,1,0:T(8,128)(2,1)S(1)} %get-tuple-element.319), channel_id=1, source_target_pairs={{0,4},{4,8},{8,12},{12,16},{16,20},{20,24},{24,28},{1,5},{5,9},{9,... | collective-permute-start | bytes 393224 | tf_op jit(solution)/shard_map/ppermute | solution.py:19
  31.3 1.0 copy-start.6
  31.3 1.1 copy-start.7
  32.4 0.8 copy-start.11
  32.4 0.8 copy-start.13
  32.4 0.8 copy-start.14
  33.2 4.9 %copy-start.5 = (bf16[2048,128]{1,0:T(8,128)(2,1)}, bf16[2048,128]{1,0:T(8,128)(2,1)S(1)}, u32[]{:S(2)}) copy-start(bf16[2048,128]{1,0:T(8,128)(2,1)S(1)} %pad_maximum_fusion) | copy-start | bytes 1572868
  38.1 4.8 %copy-start.9 = (bf16[128,256]{1,0:T(8,128)(2,1)S(1)}, bf16[128,256]{1,0:T(8,128)(2,1)}, u32[]{:S(2)}) copy-start(bf16[128,256]{1,0:T(8,128)(2,1)} %copy-done.8) | copy-start | bytes 196612
  38.1 4.8 %copy-start.16 = (f32[2048,256]{0,1:T(8,128)S(1)}, f32[2048,256]{0,1:T(8,128)}, u32[]{:S(2)}) copy-start(f32[2048,256]{0,1:T(8,128)} %get-tuple-element.328) | copy-start | bytes 6291460
  39.2 7.9 %collective-permute-start.2 = (bf16[2,2,256,128]{2,3,1,0:T(8,128)(2,1)S(1)}, bf16[2,2,256,128]{2,3,1,0:T(8,128)(2,1)S(1)}, u32[]{:S(2)}, u32[]{:S(2)}) collective-permute-start(bf16[2,2,256,128]{2,3,1,0:T(8,128)(2,1)S(1)} %pad_maximum_fusion.2), channel_id=1, source_target_pairs={{0,8},{4,12},{8,16},{12,20},{16,24},{20,28},{1,9},{5,13},{9,17},{1... | collective-permute-start | bytes 786440 | tf_op jit(solution)/shard_map/ppermute | solution.py:19
  49.3 3.9 %copy-start.3 = (f32[2048,128]{1,0:T(8,128)S(1)}, f32[2048,128]{1,0:T(8,128)}, u32[]{:S(2)}) copy-start(f32[2048,128]{1,0:T(8,128)} %get-tuple-element.409) | copy-start | bytes 3145732 | tf_op jit(solution)/shard_map/while
  51.2 1.4 %copy-start.1 = (f32[2048,256]{0,1:T(8,128)}, f32[2048,256]{0,1:T(8,128)S(1)}, u32[]{:S(2)}) copy-start(f32[2048,256]{0,1:T(8,128)S(1)} %get-tuple-element.390) | copy-start | bytes 6291460 | tf_op jit(solution)/shard_map/while
  55.9 1.0 copy-start.4
  57.3 3.9 %copy-start.3 = (f32[2048,128]{1,0:T(8,128)S(1)}, f32[2048,128]{1,0:T(8,128)}, u32[]{:S(2)}) copy-start(f32[2048,128]{1,0:T(8,128)} %get-tuple-element.409) | copy-start | bytes 3145732 | tf_op jit(solution)/shard_map/while
  59.2 1.4 %copy-start.1 = (f32[2048,256]{0,1:T(8,128)}, f32[2048,256]{0,1:T(8,128)S(1)}, u32[]{:S(2)}) copy-start(f32[2048,256]{0,1:T(8,128)S(1)} %get-tuple-element.390) | copy-start | bytes 6291460 | tf_op jit(solution)/shard_map/while
  64.0 1.0 copy-start.4
  65.4 3.9 %copy-start.3 = (f32[2048,128]{1,0:T(8,128)S(1)}, f32[2048,128]{1,0:T(8,128)}, u32[]{:S(2)}) copy-start(f32[2048,128]{1,0:T(8,128)} %get-tuple-element.409) | copy-start | bytes 3145732 | tf_op jit(solution)/shard_map/while
  67.3 1.4 %copy-start.1 = (f32[2048,256]{0,1:T(8,128)}, f32[2048,256]{0,1:T(8,128)S(1)}, u32[]{:S(2)}) copy-start(f32[2048,256]{0,1:T(8,128)S(1)} %get-tuple-element.390) | copy-start | bytes 6291460 | tf_op jit(solution)/shard_map/while
  72.0 1.0 copy-start.4
Sparse Core Ops, SparseCore 0:
  79.3 24.0 reduce-scatter.1
where the time goes:
time: 111 us; the launch traced here: 110 us
  matrix products  33.7 us (30%)
  waiting for transfers between devices  24.5 us (22%)
  between operations  13.8 us (12%)
  starting transfers between devices  13.7 us (12%)
  other arithmetic  12.2 us (11%)
  local copies, waits for them, and re-layouts  12 us (11%)
    reduce_scatter x1, waiting for transfers between devices, local(): lax.psum_scatter(head_term.astype(jnp.bfloat16), 'tp', scatter_dimension=...  24.2 us
    ppermute x3, starting transfers between devices, passed_along(): return lax.ppermute(block, axis, route)  13.7 us
    dot_general x5, matrix products, attend(): jnp.dot(weights.astype(jnp.bfloat16), kv_block[1], preferred_element_type...  12.1 us
    dot_general x5, matrix products, attend(): lax.dot_general(queries, kv_block[0], (((1,), (1,)), ((), ())), preferred...  10.5 us
    while x21, local copies, waits for them, and re-layouts  6.9 us
    dot_general x1, matrix products, local(): head_term = jnp.dot(attended, w_out, preferred_element_type=jnp.float32)  4.43 us
    dot_general x1, matrix products, local(): jnp.dot(tokens, w_query, preferred_element_type=jnp.float32)  3.43 us
    concatenate x2, other arithmetic, local(): window = jnp.concatenate([arrived, window], axis=0)  2.85 us
  transfers between devices with their start and end apart: 4, of which 2 were waited for; matrix products, arithmetic and copies ran while one was open for 16% of the time, Pallas kernels for 0%

commit v1 on v0

v1 whole, which is shorter than its diff:
```python
import functools
import math

import jax
import jax.numpy as jnp
import numpy as np
from jax import lax
from jax.experimental import pallas as pl
from jax.experimental.pallas import tpu as pltpu
from jax.sharding import PartitionSpec as P

H = 32
KVH = 4
HD = 128
EPSILON = 1e-06
ROPE_BASE = 1000000.0
HIDE = 256.0
CHUNKS = 2
MESH = pl.DeviceIdType.MESH
BF16 = jnp.bfloat16
F32 = jnp.float32


def turns_per_token():
    half = HD // 2
    freq = ROPE_BASE ** (-2.0 * np.arange(half) / HD) / (2 * math.pi)
    return np.concatenate([freq, freq])[None, :].astype(np.float32)


def cos_of_turns(turns):
    x = (turns - jnp.round(turns)) * (2 * math.pi)
    x2 = x * x
    out = jnp.full_like(x2, 1.0 / math.factorial(16))
    for n in range(14, -1, -2):
        out = out * x2 + (-1.0) ** (n // 2) / math.factorial(n)
    return out


def mm(a, b):
    return jnp.dot(a, b, preferred_element_type=F32)


def norm_rotate(u, gain, cos2, sin2):
    inv = lax.rsqrt(jnp.mean(u * u, axis=-1, keepdims=True) + EPSILON)
    w = u * inv * gain
    return w * cos2 + pltpu.roll(w, HD // 2, 1) * sin2


def kernel(
    reach, n_ctx, n_tp, docs,
    docs_ref, tok_hbm, wq_hbm, wk_hbm, wv_hbm, wo_hbm, qg_hbm, kg_hbm, fr_hbm,
    out_ref,
    tok, wkv, wq, wo, qg, kg, fr, cos2, sin2, kv, code, q_s, acc, att, s1, r1, s2, r2, own,
    in_sem, wq_sem, z_send, y_send, kv_recv, s1_send, s1_recv, s2_send, s2_recv,
):
    rows = tok.shape[0]
    heads = wq.shape[1] // HD
    wide = code.shape[2]
    chunks, qrows, _ = q_s.shape
    ct = rows // chunks
    nb = n_tp // 2
    cw = out_ref.shape[1]
    i = lax.axis_index("ctx")
    t = lax.axis_index("tp")
    pair = i + 1 - 2 * (i % 2)
    odd = i % 2 == 1
    partner = t + 1 - 2 * (t % 2)
    kv_head = t * heads // (H // KVH)

    def fetch(src, dst, sem):
        copy = pltpu.make_async_copy(src, dst, sem)
        copy.start()
        return copy

    kv_cols = pl.ds(pl.multiple_of(kv_head * HD, HD), HD)
    tok_copy = fetch(tok_hbm, tok, in_sem.at[0])
    wk_copy = fetch(wk_hbm.at[:, kv_cols], wkv.at[:, pl.ds(0, HD)], in_sem.at[1])
    wv_copy = fetch(wv_hbm.at[:, kv_cols], wkv.at[:, pl.ds(HD, HD)], in_sem.at[2])
    small = [
        fetch(fr_hbm, fr, in_sem.at[3]),
        fetch(qg_hbm, qg, in_sem.at[4]),
        fetch(kg_hbm, kg, in_sem.at[5]),
    ]
    q_parts = heads // 2
    wq_copies = [
        fetch(
            wq_hbm.at[:, pl.ds(n * 2 * HD, 2 * HD)],
            wq.at[:, pl.ds(n * 2 * HD, 2 * HD)],
            wq_sem.at[n],
        )
        for n in range(q_parts)
    ]
    wo_copy = fetch(wo_hbm, wo, in_sem.at[6])

    barrier = pltpu.get_barrier_semaphore()

    def greet(where):
        pl.semaphore_signal(barrier, inc=1, device_id=where, device_id_type=MESH)

    greet((pair, t))
    greet((i, partner))
    for step in range(1, nb):
        greet((i, (t + 2 * step) % n_tp))

    @pl.when(i >= 2)
    def _():
        greet((i - 2, t))

    @pl.when(i + 2 < n_ctx)
    def _():
        greet((i + 2, t))

    lane = lax.broadcasted_iota(jnp.int32, (1, wide), 1)

    def add_doc(d, state):
        begin, starts, ends = state
        end = begin + docs_ref[d]
        starts = jnp.where(lane == d, begin, starts)
        ends = jnp.where(lane == d, end, ends)
        return end, starts, ends

    nothing = jnp.full((1, wide), -1, jnp.int32)
    _, starts, ends = lax.fori_loop(0, docs, add_doc, (jnp.int32(0), nothing, nothing))
    local = lax.broadcasted_iota(jnp.int32, (rows, wide), 0)
    lanes = lax.broadcasted_iota(jnp.int32, (rows, wide), 1)

    def members(d):
        pos = local + (i - d) * rows
        return (pos >= starts) & (pos < ends)

    for d in range(reach + 1):
        held = jnp.where(members(d), HIDE, jnp.where(lanes == docs, -HIDE, 0.0))
        code[d] = held.astype(BF16)
    mine = members(0)
    q_code = jnp.where(mine | (lanes == docs), 1.0, 0.0).astype(BF16)
    for c in range(chunks):
        for h in range(heads):
            q_s[c, pl.ds(h * ct, ct), pl.ds(HD, wide)] = q_code[c * ct : (c + 1) * ct]
    start = jnp.sum(jnp.where(mine, starts, 0).astype(F32), axis=1, keepdims=True)
    pos = (lax.broadcasted_iota(jnp.int32, (rows, HD), 0) + i * rows).astype(F32)
    for copy in small:
        copy.wait()
    turns = (pos - start) * fr[...]
    low = lax.broadcasted_iota(jnp.int32, (rows, HD), 1) < HD // 2
    cos2[...] = cos_of_turns(turns)
    sine = cos_of_turns(turns - 0.25)
    sin2[...] = jnp.where(low, -sine, sine)

    for d in range(1, reach + 1):

        @pl.when(i < d)
        def _():
            kv[d] = jnp.zeros(kv.shape[1:], BF16)

    tok_copy.wait()
    wk_copy.wait()
    wv_copy.wait()
    projected = mm(tok[...], wkv[...])
    kv[0, 0] = norm_rotate(projected[:, :HD], kg[...], cos2[...], sin2[...]).astype(BF16)
    kv[0, 1] = projected[:, HD:].astype(BF16)

    greeted = 1 + nb + jnp.where(i >= 2, 1, 0) + jnp.where(i + 2 < n_ctx, 1, 0)
    pl.semaphore_wait(barrier, greeted)

    def hop(src, dst, piece, where, sems):
        return pltpu.make_async_remote_copy(
            src_ref=kv.at[src, piece],
            dst_ref=kv.at[dst, piece],
            send_sem=sems.at[src // 2, piece],
            recv_sem=kv_recv.at[dst, piece],
            device_id=(where, t),
            device_id_type=MESH,
        )

    def hops(d, piece):
        there = i >= d
        moves = []
        if d + 2 <= reach:
            moves.append((there & (i + 2 < n_ctx), hop(d, d + 2, piece, i + 2, z_send)))
        if d + 1 <= reach:
            moves.append((there & jnp.logical_not(odd), hop(d, d + 1, piece, pair, y_send)))
        if d >= 2:
            moves.append((there & odd, hop(d, d - 1, piece, pair, y_send)))
        return moves

    def forward(d):
        for piece in range(2):
            if d:
                arrive(d, piece)
            for cond, copy in hops(d, piece):

                @pl.when(cond)
                def _():
                    copy.start()

    def arrive(d, piece):
        @pl.when(i >= d)
        def _():
            hop(0, d, piece, pair, z_send).wait_recv()

    forward(0)

    scale = HD ** (-0.5) * math.log2(math.e)

    for n in range(q_parts):
        wq_copies[n].wait()

    def project(n, _):
        cols = pl.ds(pl.multiple_of(n * 2 * HD, 2 * HD), 2 * HD)
        both = mm(tok[...], wq[:, cols])
        for k in range(2):
            one = norm_rotate(both[:, k * HD : (k + 1) * HD], qg[...] * scale, cos2[...], sin2[...])
            one = one.astype(BF16)
            at = pl.multiple_of((n * 2 + k) * ct, ct)
            for c in range(chunks):
                q_s[c, pl.ds(at, ct), pl.ds(0, HD)] = one[c * ct : (c + 1) * ct]
        return 0

    lax.fori_loop(0, q_parts, project, 0)
    forward(2)

    group = min(4, heads)
    grows = group * ct
    groups = heads // group
    ones = jnp.ones((rows, HD), BF16)

    def weights_of(c, at, d):
        keys = jnp.concatenate([kv[d, 0], code[d]], axis=1)
        scores = lax.dot_general(
            q_s[c, pl.ds(at, grows), :], keys, (((1,), (1,)), ((), ())), preferred_element_type=F32
        )
        weights = jnp.exp2(scores)
        if d == 0:
            token = lax.broadcasted_iota(jnp.int32, (ct, rows), 0) + c * ct
            seen = lax.broadcasted_iota(jnp.int32, (ct, rows), 1) <= token
            weights = jnp.where(seen[None], weights.reshape(group, ct, rows), 0.0)
            weights = weights.reshape(grows, rows)
        return weights.astype(BF16)

    def weighted(c, at, d):
        return mm(weights_of(c, at, d), jnp.concatenate([kv[d, 1], ones], axis=1))

    def attend(d):
        def step(n, _):
            c = n // groups
            at = pl.multiple_of((n % groups) * grows, grows)
            new = weighted(c, at, d)
            if d == 0:
                acc[c, pl.ds(at, grows), :] = new
            else:
                acc[c, pl.ds(at, grows), :] += new
            return 0

        lax.fori_loop(0, chunks * groups, step, 0)

    attend(0)
    for d in range(2, reach, 2):
        attend(d)
        forward(d + 2)
    for d in range(1, reach - 1, 2):
        for piece in range(2):
            arrive(d, piece)
        attend(d)
    for piece in range(2):
        arrive(reach - 1, piece)

    wo_copy.wait()

    def pair_copy(c, k):
        return pltpu.make_async_remote_copy(
            src_ref=s1.at[c, k],
            dst_ref=r1.at[c, k],
            send_sem=s1_send.at[c, k],
            recv_sem=s1_recv.at[c, k],
            device_id=(i, partner),
            device_id_type=MESH,
        )

    def chip_copy(c, k):
        return pltpu.make_async_remote_copy(
            src_ref=s2.at[c, k - 1],
            dst_ref=r2.at[c, k - 1],
            send_sem=s2_send.at[c, k - 1],
            recv_sem=s2_recv.at[c, k - 1],
            device_id=(i, (t + 2 * k) % n_tp),
            device_id_type=MESH,
        )

    def columns(owner):
        return pl.ds(pl.multiple_of(owner * cw, cw), cw)

    for c in range(chunks):

        def finish(n, _):
            at = pl.multiple_of(n * grows, grows)
            total = acc[c, pl.ds(at, grows), :]
            total = total + weighted(c, at, reach) + weighted(c, at, reach - 1)
            done = (total[:, :HD] / total[:, HD:]).astype(BF16)
            for h in range(group):
                cols = pl.ds(pl.multiple_of(n * group * HD + h * HD, HD), HD)
                att[c, :, cols] = done[h * ct : (h + 1) * ct]
            return 0

        lax.fori_loop(0, groups, finish, 0)
        order = list(range(1, nb)) + [0]
        for k in order:
            s1[c, k] = mm(att[c], wo[:, columns((partner + 2 * k) % n_tp)]).astype(BF16)
            pair_copy(c, k).start()
        for k in order:
            term = mm(att[c], wo[:, columns((t + 2 * k) % n_tp)]).astype(BF16).astype(F32)
            pair_copy(c, k).wait_recv()
            term = term + r1[c, k].astype(F32)
            if k:
                s2[c, k - 1] = term.astype(BF16)
                chip_copy(c, k).start()
            else:
                own[c] = term

    for c in range(chunks):
        total = own[c]
        for k in range(1, nb):
            chip_copy(c, k).wait_recv()
            total = total + r2[c, k - 1].astype(F32)
        out_ref[pl.ds(c * ct, ct), :] = total.astype(out_ref.dtype)

    for c in range(chunks):
        for k in range(nb):
            pair_copy(c, k).wait_send()
            if k:
                chip_copy(c, k).wait_send()
    for d in range(0, reach + 1, 2):
        for piece in range(2):
            for cond, copy in hops(d, piece):

                @pl.when(cond)
                def _():
                    copy.wait_send()


def local(n_ctx, n_tp, tokens, w_query, w_key, w_value, w_out, query_gain, key_gain, doc_lengths):
    rows, width = tokens.shape
    heads = w_query.shape[1] // HD
    out_width = w_out.shape[1]
    reach = min(16, n_ctx // 2)
    docs = doc_lengths.shape[0]
    wide = -(-(docs + 1) // 128) * 128
    chunks = CHUNKS
    ct = rows // chunks
    nb = n_tp // 2
    cw = out_width // n_tp
    dma = pltpu.SemaphoreType.DMA
    anywhere = pl.BlockSpec(memory_space=pl.ANY)
    macs = rows * width * (heads + 2) * HD + rows * heads * HD * out_width
    macs += 2 * rows * heads * rows * (reach + 1) * 2 * HD
    return pl.pallas_call(
        functools.partial(kernel, reach, n_ctx, n_tp, docs),
        out_shape=jax.ShapeDtypeStruct((rows, cw), BF16),
        in_specs=[pl.BlockSpec(memory_space=pltpu.SMEM)] + [anywhere] * 8,
        out_specs=pl.BlockSpec(memory_space=pltpu.VMEM),
        scratch_shapes=[
            pltpu.VMEM((rows, width), BF16),
            pltpu.VMEM((width, 2 * HD), BF16),
            pltpu.VMEM((width, heads * HD), BF16),
            pltpu.VMEM((heads * HD, out_width), BF16),
            pltpu.VMEM((1, HD), F32),
            pltpu.VMEM((1, HD), F32),
            pltpu.VMEM((1, HD), F32),
            pltpu.VMEM((rows, HD), F32),
            pltpu.VMEM((rows, HD), F32),
            pltpu.VMEM((reach + 1, 2, rows, HD), BF16),
            pltpu.VMEM((reach + 1, rows, wide), BF16),
            pltpu.VMEM((chunks, heads * ct, HD + wide), BF16),
            pltpu.VMEM((chunks, heads * ct, 2 * HD), F32),
            pltpu.VMEM((chunks, ct, heads * HD), BF16),
            pltpu.VMEM((chunks, nb, ct, cw), BF16),
            pltpu.VMEM((chunks, nb, ct, cw), BF16),
            pltpu.VMEM((chunks, nb - 1, ct, cw), BF16),
            pltpu.VMEM((chunks, nb - 1, ct, cw), BF16),
            pltpu.VMEM((chunks, ct, cw), F32),
            dma((7,)),
            dma((heads // 2,)),
            dma((reach // 2 + 1, 2)),
            dma((reach // 2 + 1, 2)),
            dma((reach + 1, 2)),
            dma((chunks, nb)),
            dma((chunks, nb)),
            dma((chunks, nb - 1)),
            dma((chunks, nb - 1)),
        ],
        compiler_params=pltpu.CompilerParams(
            collective_id=0, has_side_effects=True, vmem_limit_bytes=48 * 2**20
        ),
        cost_estimate=pl.CostEstimate(
            flops=2 * macs,
            bytes_accessed=2 * (tokens.size + w_query.size + w_out.size + 2 * width * HD),
            transcendentals=rows * heads * rows * (reach + 1),
        ),
        name="attention_layer",
    )(
        doc_lengths, tokens, w_query, w_key, w_value, w_out,
        query_gain.reshape(1, HD), key_gain.reshape(1, HD), jnp.asarray(turns_per_token()),
    )


def solution(mesh):
    return jax.shard_map(
        functools.partial(local, mesh.shape["ctx"], mesh.shape["tp"]),
        mesh=mesh,
        in_specs=(P("ctx", None), P(None, "tp"), P(), P(), P("tp", None), P(), P(), P()),
        out_specs=P("ctx", "tp"),
        check_vma=False,
    )
```

time: 111 us -> 33.6 us (0.30)
  the two profiles are of different devices: /device:TPU:0 before, /device:TPU:16 now
where the time goes in v1:
time: 33.6 us; the launch traced here: 33.4 us
  Pallas kernels  25.6 us (76%)
  local copies, waits for them, and re-layouts  7.73 us (23%)
    pallas_call x1, Pallas kernels, local(): pl.pallas_call(functools.partial(kernel, reach, n_ctx, n_tp, docs), out_s...  25.6 us
    unnamed x15, local copies, waits for them, and re-layouts  7.73 us

profile of v1, /device:TPU:16, one launch (start us, length us, event | category | flops | bytes accessed | tf_op | source)
XLA Modules:
  0.0 33.4 jit_solution(9095969826064421261)
XLA Ops:
  0.0 0.0 copy-start
  0.0 1.6 %copy-done = bf16[2048,512]{1,0:T(8,128)(2,1)S(1)} copy-done((bf16[2048,512]{1,0:T(8,128)(2,1)S(1)}, bf16[2048,512]{1,0:T(8,128)(2,1)}, u32[]{:S(2)}) %copy-start) | copy-done | bytes 2097176
  1.6 0.0 copy-start.1
  1.6 1.6 %copy-done.1 = bf16[2048,512]{1,0:T(8,128)(2,1)S(1)} copy-done((bf16[2048,512]{1,0:T(8,128)(2,1)S(1)}, bf16[2048,512]{1,0:T(8,128)(2,1)}, u32[]{:S(2)}) %copy-start.1) | copy-done | bytes 2097176
  3.2 0.0 copy-start.2
  3.2 1.2 %copy-done.2 = bf16[256,2048]{1,0:T(8,128)(2,1)S(1)} copy-done((bf16[256,2048]{1,0:T(8,128)(2,1)S(1)}, bf16[256,2048]{1,0:T(8,128)(2,1)}, u32[]{:S(2)}) %copy-start.2) | copy-done | bytes 1048600
  4.4 0.0 copy-start.3
  4.4 0.7 %copy-done.3 = s32[16]{0:T(128)S(1)} copy-done((s32[16]{0:T(128)S(1)}, s32[16]{0:T(128)}, u32[]{:S(2)}) %copy-start.3) | copy-done | bytes 88
  5.1 0.0 copy-start.4
  5.1 0.7 %copy-done.4 = f32[128]{0:T(128)S(1)} copy-done((f32[128]{0:T(128)S(1)}, f32[128]{0:T(128)}, u32[]{:S(2)}) %copy-start.4) | copy-done | bytes 536
  5.7 0.0 copy-start.5
  5.7 0.7 %copy-done.5 = f32[128]{0:T(128)S(1)} copy-done((f32[128]{0:T(128)S(1)}, f32[128]{0:T(128)}, u32[]{:S(2)}) %copy-start.5) | copy-done | bytes 536
  6.4 0.0 copy-start.6
  6.4 0.7 %copy-done.6 = f32[1,128]{1,0:T(1,128)S(1)} copy-done((f32[1,128]{1,0:T(1,128)S(1)}, f32[1,128]{1,0:T(1,128)}, u32[]{:S(2)}) %copy-start.6) | copy-done | bytes 536
  7.0 25.6 %attention_layer.1 = bf16[256,512]{1,0:T(8,128)(2,1)S(1)} custom-call(s32[16]{0:T(128)S(1)} %copy-done.3, bf16[256,2048]{1,0:T(8,128)(2,1)S(1)} %copy-done.2, bf16[2048,1024]{1,0:T(8,128)(2,1)} %wq_hbm.1, bf16[2048,512]{1,0:T(8,128)(2,1)S(1)} %copy-done, bf16[2048,512]{1,0:T(8,128)(2,1)S(1)} %copy-done.1, bf16[1024,2048]{1,0:T(8,128)(2,1)} %wo_hbm.1, ...), custom_call_target="tpu_custom_call" | custom-call | flops 5100273664 | bytes 10485760 | tf_op jit(solution)/shard_map/attention_layer/pallas_call | solution.py:355
  32.7 0.7 %copy.11 = bf16[256,512]{1,0:T(8,128)(2,1)} copy(bf16[256,512]{1,0:T(8,128)(2,1)S(1)} %attention_layer.1) | data formatting | bytes 524288
Async XLA Ops:
  0.0 1.6 %copy-start = (bf16[2048,512]{1,0:T(8,128)(2,1)S(1)}, bf16[2048,512]{1,0:T(8,128)(2,1)}, u32[]{:S(2)}) copy-start(bf16[2048,512]{1,0:T(8,128)(2,1)} %wk_hbm.1) | copy-start | bytes 6291460
  1.6 1.6 %copy-start.1 = (bf16[2048,512]{1,0:T(8,128)(2,1)S(1)}, bf16[2048,512]{1,0:T(8,128)(2,1)}, u32[]{:S(2)}) copy-start(bf16[2048,512]{1,0:T(8,128)(2,1)} %wv_hbm.1) | copy-start | bytes 6291460
  3.2 1.2 %copy-start.2 = (bf16[256,2048]{1,0:T(8,128)(2,1)S(1)}, bf16[256,2048]{1,0:T(8,128)(2,1)}, u32[]{:S(2)}) copy-start(bf16[256,2048]{1,0:T(8,128)(2,1)} %tok_hbm.1) | copy-start | bytes 3145732
  4.4 0.7 %copy-start.3 = (s32[16]{0:T(128)S(1)}, s32[16]{0:T(128)}, u32[]{:S(2)}) copy-start(s32[16]{0:T(128)} %docs_ref.1) | copy-start | bytes 196
  5.1 0.7 %copy-start.4 = (f32[128]{0:T(128)S(1)}, f32[128]{0:T(128)}, u32[]{:S(2)}) copy-start(f32[128]{0:T(128)} %param.14) | copy-start | bytes 1540
  5.7 0.7 %copy-start.5 = (f32[128]{0:T(128)S(1)}, f32[128]{0:T(128)}, u32[]{:S(2)}) copy-start(f32[128]{0:T(128)} %param.15) | copy-start | bytes 1540
  6.4 0.7 %copy-start.6 = (f32[1,128]{1,0:T(1,128)S(1)}, f32[1,128]{1,0:T(1,128)}, u32[]{:S(2)}) copy-start(f32[1,128]{1,0:T(1,128)} %constant.2.clone.fr_hbm) | copy-start | bytes 1540

commit v2 on v1

--- a/solution.py
+++ b/solution.py
@@ -16,6 +16,7 @@
 ROPE_BASE = 1000000.0
 HIDE = 256.0
 CHUNKS = 2
+PIECES = 4
 MESH = pl.DeviceIdType.MESH
 BF16 = jnp.bfloat16
 F32 = jnp.float32
@@ -128,14 +129,7 @@
         pos = local + (i - d) * rows
         return (pos >= starts) & (pos < ends)
 
-    for d in range(reach + 1):
-        held = jnp.where(members(d), HIDE, jnp.where(lanes == docs, -HIDE, 0.0))
-        code[d] = held.astype(BF16)
     mine = members(0)
-    q_code = jnp.where(mine | (lanes == docs), 1.0, 0.0).astype(BF16)
-    for c in range(chunks):
-        for h in range(heads):
-            q_s[c, pl.ds(h * ct, ct), pl.ds(HD, wide)] = q_code[c * ct : (c + 1) * ct]
     start = jnp.sum(jnp.where(mine, starts, 0).astype(F32), axis=1, keepdims=True)
     pos = (lax.broadcasted_iota(jnp.int32, (rows, HD), 0) + i * rows).astype(F32)
     for copy in small:
@@ -146,12 +140,6 @@
     sine = cos_of_turns(turns - 0.25)
     sin2[...] = jnp.where(low, -sine, sine)
 
-    for d in range(1, reach + 1):
-
-        @pl.when(i < d)
-        def _():
-            kv[d] = jnp.zeros(kv.shape[1:], BF16)
-
     tok_copy.wait()
     wk_copy.wait()
     wv_copy.wait()
@@ -162,10 +150,13 @@
     greeted = 1 + nb + jnp.where(i >= 2, 1, 0) + jnp.where(i + 2 < n_ctx, 1, 0)
     pl.semaphore_wait(barrier, greeted)
 
+    part = rows // PIECES
+
     def hop(src, dst, piece, where, sems):
+        here = (slice(None), pl.ds(piece * part, part), slice(None))
         return pltpu.make_async_remote_copy(
-            src_ref=kv.at[src, piece],
-            dst_ref=kv.at[dst, piece],
+            src_ref=kv.at[(src,) + here],
+            dst_ref=kv.at[(dst,) + here],
             send_sem=sems.at[src // 2, piece],
             recv_sem=kv_recv.at[dst, piece],
             device_id=(where, t),
@@ -183,8 +174,8 @@
             moves.append((there & odd, hop(d, d - 1, piece, pair, y_send)))
         return moves
 
-    def forward(d):
-        for piece in range(2):
+    def forward(d, pieces):
+        for piece in pieces:
             if d:
                 arrive(d, piece)
             for cond, copy in hops(d, piece):
@@ -198,12 +189,23 @@
         def _():
             hop(0, d, piece, pair, z_send).wait_recv()
 
-    forward(0)
+    every = range(PIECES)
+    forward(0, every)
+
+    for d in range(reach + 1):
+        held = jnp.where(members(d), HIDE, jnp.where(lanes == docs, -HIDE, 0.0))
+        code[d] = held.astype(BF16)
+    q_code = jnp.where(mine | (lanes == docs), 1.0, 0.0).astype(BF16)
+    for c in range(chunks):
+        for h in range(heads):
+            q_s[c, pl.ds(h * ct, ct), pl.ds(HD, wide)] = q_code[c * ct : (c + 1) * ct]
+    for d in range(1, reach + 1):
+
+        @pl.when(i < d)
+        def _():
+            kv[d] = jnp.zeros(kv.shape[1:], BF16)
 
     scale = HD ** (-0.5) * math.log2(math.e)
-
-    for n in range(q_parts):
-        wq_copies[n].wait()
 
     def project(n, _):
         cols = pl.ds(pl.multiple_of(n * 2 * HD, 2 * HD), 2 * HD)
@@ -216,8 +218,17 @@
                 q_s[c, pl.ds(at, ct), pl.ds(0, HD)] = one[c * ct : (c + 1) * ct]
         return 0
 
-    lax.fori_loop(0, q_parts, project, 0)
-    forward(2)
+    early = q_parts - 2
+    for n in range(early):
+        wq_copies[n].wait()
+    lax.fori_loop(0, early, project, 0)
+    forward(2, every[:1])
+    wq_copies[early].wait()
+    project(early, 0)
+    forward(2, every[1:2])
+    wq_copies[early + 1].wait()
+    project(early + 1, 0)
+    forward(2, every[2:])
 
     group = min(4, heads)
     grows = group * ct
@@ -253,15 +264,19 @@
 
         lax.fori_loop(0, chunks * groups, step, 0)
 
+    forward(4, every[:1])
     attend(0)
-    for d in range(2, reach, 2):
-        attend(d)
-        forward(d + 2)
+    forward(4, every[1:])
+    attend(2)
+    for d in range(6, reach + 1, 2):
+        forward(d, every)
+        attend(d - 2)
     for d in range(1, reach - 1, 2):
-        for piece in range(2):
+        for piece in every:
             arrive(d, piece)
         attend(d)
-    for piece in range(2):
+    attend(reach)
+    for piece in every:
         arrive(reach - 1, piece)
 
     wo_copy.wait()
@@ -294,7 +309,7 @@
         def finish(n, _):
             at = pl.multiple_of(n * grows, grows)
             total = acc[c, pl.ds(at, grows), :]
-            total = total + weighted(c, at, reach) + weighted(c, at, reach - 1)
+            total = total + weighted(c, at, reach - 1)
             done = (total[:, :HD] / total[:, HD:]).astype(BF16)
             for h in range(group):
                 cols = pl.ds(pl.multiple_of(n * group * HD + h * HD, HD), HD)
@@ -329,7 +344,7 @@
             if k:
                 chip_copy(c, k).wait_send()
     for d in range(0, reach + 1, 2):
-        for piece in range(2):
+        for piece in every:
             for cond, copy in hops(d, piece):
 
                 @pl.when(cond)
@@ -349,7 +364,7 @@
     nb = n_tp // 2
     cw = out_width // n_tp
     dma = pltpu.SemaphoreType.DMA
-    anywhere = pl.BlockSpec(memory_space=pl.ANY)
+    anywhere = pl.BlockSpec(memory_space=pltpu.HBM)
     macs = rows * width * (heads + 2) * HD + rows * heads * HD * out_width
     macs += 2 * rows * heads * rows * (reach + 1) * 2 * HD
     return pl.pallas_call(
@@ -379,16 +394,16 @@
             pltpu.VMEM((chunks, ct, cw), F32),
             dma((7,)),
             dma((heads // 2,)),
-            dma((reach // 2 + 1, 2)),
-            dma((reach // 2 + 1, 2)),
-            dma((reach + 1, 2)),
+            dma((reach // 2 + 1, PIECES)),
+            dma((reach // 2 + 1, PIECES)),
+            dma((reach + 1, PIECES)),
             dma((chunks, nb)),
             dma((chunks, nb)),
             dma((chunks, nb - 1)),
             dma((chunks, nb - 1)),
         ],
         compiler_params=pltpu.CompilerParams(
-            collective_id=0, has_side_effects=True, vmem_limit_bytes=48 * 2**20
+            collective_id=0, has_side_effects=True, vmem_limit_bytes=64 * 2**20
         ),
         cost_estimate=pl.CostEstimate(
             flops=2 * macs,

time: 33.6 us -> 29.8 us (0.89)
  local copies, waits for them, and re-layouts: 7.73 us -> 1.67 us
  Pallas kernels: 25.6 us -> 27.9 us
    unnamed x15 -> x1, local copies, waits for them, and re-layouts: 7.73 us -> 1.67 us
    pallas_call x1, Pallas kernels: 25.6 us -> 27.9 us  [local(): pl.pallas_call(functools.partial(kernel, reach, n_ctx, n_tp, docs), out_s...]
where the time goes in v2:
time: 29.8 us; the launch traced here: 29.6 us
  Pallas kernels  27.9 us (94%)
  local copies, waits for them, and re-layouts  1.67 us (6%)
    pallas_call x1, Pallas kernels, local(): pl.pallas_call(functools.partial(kernel, reach, n_ctx, n_tp, docs), out_s...  27.9 us
    unnamed x1, local copies, waits for them, and re-layouts  1.67 us

profile of v2, /device:TPU:16, one launch (start us, length us, event | category | flops | bytes accessed | tf_op | source)
XLA Modules:
  0.0 29.6 jit_solution(7290049019291485264)
XLA Ops:
  0.0 27.9 %attention_layer.1 = bf16[256,512]{1,0:T(8,128)(2,1)} custom-call(s32[16]{0:T(128)} %docs_ref.1, bf16[256,2048]{1,0:T(8,128)(2,1)} %tok_hbm.1, bf16[2048,1024]{1,0:T(8,128)(2,1)} %wq_hbm.1, bf16[2048,512]{1,0:T(8,128)(2,1)} %wk_hbm.1, bf16[2048,512]{1,0:T(8,128)(2,1)} %wv_hbm.1, bf16[1024,2048]{1,0:T(8,128)(2,1)} %wo_hbm.1, f32[1,128]{1,0:T(1,128)} %bitcast.2, ...), custom_call_target="tpu_custom_call" | custom-call | flops 5100273664 | bytes 10485760 | tf_op jit(solution)/shard_map/attention_layer/pallas_call | solution.py:370
  27.9 1.7 %copy.11 = bf16[256,512]{1,0:T(8,128)(2,1)} copy(bf16[256,512]{1,0:T(8,128)(2,1)} %attention_layer.1) | data formatting | bytes 524288

commit v3 on v2

--- a/solution.py
+++ b/solution.py
@@ -15,8 +15,9 @@
 EPSILON = 1e-06
 ROPE_BASE = 1000000.0
 HIDE = 256.0
-CHUNKS = 2
+CHUNKS = 4
 PIECES = 4
+LOADS = 4
 MESH = pl.DeviceIdType.MESH
 BF16 = jnp.bfloat16
 F32 = jnp.float32
@@ -49,18 +50,18 @@
 
 def kernel(
     reach, n_ctx, n_tp, docs,
-    docs_ref, tok_hbm, wq_hbm, wk_hbm, wv_hbm, wo_hbm, qg_hbm, kg_hbm, fr_hbm,
-    out_ref,
-    tok, wkv, wq, wo, qg, kg, fr, cos2, sin2, kv, code, q_s, acc, att, s1, r1, s2, r2, own,
-    in_sem, wq_sem, z_send, y_send, kv_recv, s1_send, s1_recv, s2_send, s2_recv,
+    docs_hbm, tok_hbm, wq_hbm, wk_hbm, wv_hbm, wo_hbm, qg_hbm, kg_hbm, fr_hbm,
+    mine_ref, r2,
+    docs_ref, tok, wkv, wq, wo, qg, kg, fr, cos2, sin2, kv, kt, q_s, acc, att, s1, r1, s2, own,
+    in_sem, tok_sem, wq_sem, own_sem, z_send, y_send, kv_recv, s1_send, s1_recv, s2_send, s2_recv,
 ):
     rows = tok.shape[0]
     heads = wq.shape[1] // HD
-    wide = code.shape[2]
+    wide = kt.shape[1] - HD
     chunks, qrows, _ = q_s.shape
     ct = rows // chunks
     nb = n_tp // 2
-    cw = out_ref.shape[1]
+    cw = mine_ref.shape[1]
     i = lax.axis_index("ctx")
     t = lax.axis_index("tp")
     pair = i + 1 - 2 * (i % 2)
@@ -74,14 +75,19 @@
         return copy
 
     kv_cols = pl.ds(pl.multiple_of(kv_head * HD, HD), HD)
-    tok_copy = fetch(tok_hbm, tok, in_sem.at[0])
-    wk_copy = fetch(wk_hbm.at[:, kv_cols], wkv.at[:, pl.ds(0, HD)], in_sem.at[1])
-    wv_copy = fetch(wv_hbm.at[:, kv_cols], wkv.at[:, pl.ds(HD, HD)], in_sem.at[2])
     small = [
-        fetch(fr_hbm, fr, in_sem.at[3]),
-        fetch(qg_hbm, qg, in_sem.at[4]),
-        fetch(kg_hbm, kg, in_sem.at[5]),
+        fetch(docs_hbm, docs_ref, in_sem.at[0]),
+        fetch(fr_hbm, fr, in_sem.at[1]),
+        fetch(qg_hbm, qg, in_sem.at[2]),
+        fetch(kg_hbm, kg, in_sem.at[3]),
     ]
+    first = []
+    for n in range(LOADS):
+        some = pl.ds(n * (rows // LOADS), rows // LOADS)
+        first.append(fetch(tok_hbm.at[some], tok.at[some], tok_sem.at[0, n]))
+        deep = pl.ds(n * (wkv.shape[0] // LOADS), wkv.shape[0] // LOADS)
+        first.append(fetch(wk_hbm.at[deep, kv_cols], wkv.at[deep, pl.ds(0, HD)], tok_sem.at[1, n]))
+        first.append(fetch(wv_hbm.at[deep, kv_cols], wkv.at[deep, pl.ds(HD, HD)], tok_sem.at[2, n]))
     q_parts = heads // 2
     wq_copies = [
         fetch(
@@ -91,7 +97,6 @@
         )
         for n in range(q_parts)
     ]
-    wo_copy = fetch(wo_hbm, wo, in_sem.at[6])
 
     barrier = pltpu.get_barrier_semaphore()
 
@@ -112,6 +117,8 @@
         greet((i + 2, t))
 
     lane = lax.broadcasted_iota(jnp.int32, (1, wide), 1)
+
+    small[0].wait()
 
     def add_doc(d, state):
         begin, starts, ends = state
@@ -132,7 +139,7 @@
     mine = members(0)
     start = jnp.sum(jnp.where(mine, starts, 0).astype(F32), axis=1, keepdims=True)
     pos = (lax.broadcasted_iota(jnp.int32, (rows, HD), 0) + i * rows).astype(F32)
-    for copy in small:
+    for copy in small[1:]:
         copy.wait()
     turns = (pos - start) * fr[...]
     low = lax.broadcasted_iota(jnp.int32, (rows, HD), 1) < HD // 2
@@ -140,9 +147,8 @@
     sine = cos_of_turns(turns - 0.25)
     sin2[...] = jnp.where(low, -sine, sine)
 
-    tok_copy.wait()
-    wk_copy.wait()
-    wv_copy.wait()
+    for copy in first:
+        copy.wait()
     projected = mm(tok[...], wkv[...])
     kv[0, 0] = norm_rotate(projected[:, :HD], kg[...], cos2[...], sin2[...]).astype(BF16)
     kv[0, 1] = projected[:, HD:].astype(BF16)
@@ -191,10 +197,17 @@
 
     every = range(PIECES)
     forward(0, every)
+    deep = heads * HD // LOADS
+    wo_copies = [
+        fetch(
+            wo_hbm.at[pl.ds(n * deep, deep)], wo.at[pl.ds(n * deep, deep)], in_sem.at[4 + n]
+        )
+        for n in range(LOADS)
+    ]
 
     for d in range(reach + 1):
         held = jnp.where(members(d), HIDE, jnp.where(lanes == docs, -HIDE, 0.0))
-        code[d] = held.astype(BF16)
+        kt[d, pl.ds(HD, wide), :] = held.T.astype(BF16)
     q_code = jnp.where(mine | (lanes == docs), 1.0, 0.0).astype(BF16)
     for c in range(chunks):
         for h in range(heads):
@@ -230,17 +243,13 @@
     project(early + 1, 0)
     forward(2, every[2:])
 
-    group = min(4, heads)
+    group = min(8, heads)
     grows = group * ct
     groups = heads // group
     ones = jnp.ones((rows, HD), BF16)
 
     def weights_of(c, at, d):
-        keys = jnp.concatenate([kv[d, 0], code[d]], axis=1)
-        scores = lax.dot_general(
-            q_s[c, pl.ds(at, grows), :], keys, (((1,), (1,)), ((), ())), preferred_element_type=F32
-        )
-        weights = jnp.exp2(scores)
+        weights = jnp.exp2(mm(q_s[c, pl.ds(at, grows), :], kt[d]))
         if d == 0:
             token = lax.broadcasted_iota(jnp.int32, (ct, rows), 0) + c * ct
             seen = lax.broadcasted_iota(jnp.int32, (ct, rows), 1) <= token
@@ -251,7 +260,12 @@
     def weighted(c, at, d):
         return mm(weights_of(c, at, d), jnp.concatenate([kv[d, 1], ones], axis=1))
 
+    def turn(d):
+        kt[d, pl.ds(0, HD), :] = kv[d, 0].astype(F32).T.astype(BF16)
+
     def attend(d):
+        turn(d)
+
         def step(n, _):
             c = n // groups
             at = pl.multiple_of((n % groups) * grows, grows)
@@ -275,11 +289,13 @@
         for piece in every:
             arrive(d, piece)
         attend(d)
-    attend(reach)
+    turn(reach)
     for piece in every:
         arrive(reach - 1, piece)
-
-    wo_copy.wait()
+    turn(reach - 1)
+
+    for copy in wo_copies:
+        copy.wait()
 
     def pair_copy(c, k):
         return pltpu.make_async_remote_copy(
@@ -294,13 +310,16 @@
     def chip_copy(c, k):
         return pltpu.make_async_remote_copy(
             src_ref=s2.at[c, k - 1],
-            dst_ref=r2.at[c, k - 1],
+            dst_ref=r2.at[k - 1, pl.ds(c * ct, ct)],
             send_sem=s2_send.at[c, k - 1],
             recv_sem=s2_recv.at[c, k - 1],
             device_id=(i, (t + 2 * k) % n_tp),
             device_id_type=MESH,
         )
 
+    def kept(c):
+        return pltpu.make_async_copy(own.at[c], mine_ref.at[pl.ds(c * ct, ct)], own_sem.at[c])
+
     def columns(owner):
         return pl.ds(pl.multiple_of(owner * cw, cw), cw)
 
@@ -309,7 +328,7 @@
         def finish(n, _):
             at = pl.multiple_of(n * grows, grows)
             total = acc[c, pl.ds(at, grows), :]
-            total = total + weighted(c, at, reach - 1)
+            total = total + weighted(c, at, reach) + weighted(c, at, reach - 1)
             done = (total[:, :HD] / total[:, HD:]).astype(BF16)
             for h in range(group):
                 cols = pl.ds(pl.multiple_of(n * group * HD + h * HD, HD), HD)
@@ -330,13 +349,12 @@
                 chip_copy(c, k).start()
             else:
                 own[c] = term
+                kept(c).start()
 
     for c in range(chunks):
-        total = own[c]
+        kept(c).wait()
         for k in range(1, nb):
             chip_copy(c, k).wait_recv()
-            total = total + r2[c, k - 1].astype(F32)
-        out_ref[pl.ds(c * ct, ct), :] = total.astype(out_ref.dtype)
 
     for c in range(chunks):
         for k in range(nb):
@@ -367,12 +385,16 @@
     anywhere = pl.BlockSpec(memory_space=pltpu.HBM)
     macs = rows * width * (heads + 2) * HD + rows * heads * HD * out_width
     macs += 2 * rows * heads * rows * (reach + 1) * 2 * HD
-    return pl.pallas_call(
+    mine, others = pl.pallas_call(
         functools.partial(kernel, reach, n_ctx, n_tp, docs),
-        out_shape=jax.ShapeDtypeStruct((rows, cw), BF16),
-        in_specs=[pl.BlockSpec(memory_space=pltpu.SMEM)] + [anywhere] * 8,
-        out_specs=pl.BlockSpec(memory_space=pltpu.VMEM),
+        out_shape=(
+            jax.ShapeDtypeStruct((rows, cw), F32),
+            jax.ShapeDtypeStruct((nb - 1, rows, cw), BF16),
+        ),
+        in_specs=[anywhere] * 9,
+        out_specs=(anywhere, anywhere),
         scratch_shapes=[
+            pltpu.SMEM((docs,), jnp.int32),
             pltpu.VMEM((rows, width), BF16),
             pltpu.VMEM((width, 2 * HD), BF16),
             pltpu.VMEM((width, heads * HD), BF16),
@@ -383,17 +405,18 @@
             pltpu.VMEM((rows, HD), F32),
             pltpu.VMEM((rows, HD), F32),
             pltpu.VMEM((reach + 1, 2, rows, HD), BF16),
-            pltpu.VMEM((reach + 1, rows, wide), BF16),
+            pltpu.VMEM((reach + 1, HD + wide, rows), BF16),
             pltpu.VMEM((chunks, heads * ct, HD + wide), BF16),
             pltpu.VMEM((chunks, heads * ct, 2 * HD), F32),
             pltpu.VMEM((chunks, ct, heads * HD), BF16),
             pltpu.VMEM((chunks, nb, ct, cw), BF16),
             pltpu.VMEM((chunks, nb, ct, cw), BF16),
             pltpu.VMEM((chunks, nb - 1, ct, cw), BF16),
-            pltpu.VMEM((chunks, nb - 1, ct, cw), BF16),
             pltpu.VMEM((chunks, ct, cw), F32),
-            dma((7,)),
+            dma((4 + LOADS,)),
+            dma((3, LOADS)),
             dma((heads // 2,)),
+            dma((chunks,)),
             dma((reach // 2 + 1, PIECES)),
             dma((reach // 2 + 1, PIECES)),
             dma((reach + 1, PIECES)),
@@ -415,6 +438,7 @@
         doc_lengths, tokens, w_query, w_key, w_value, w_out,
         query_gain.reshape(1, HD), key_gain.reshape(1, HD), jnp.asarray(turns_per_token()),
     )
+    return (mine + jnp.sum(others.astype(F32), axis=0)).astype(BF16)
 
 
 def solution(mesh):

time: 29.8 us -> 29.3 us (0.983)
  other arithmetic: 0 us -> 1.88 us
  local copies, waits for them, and re-layouts: 1.67 us -> 0 us
  Pallas kernels: 27.9 us -> 27.3 us
    convert_element_type x0 -> x1, other arithmetic: none -> 1.88 us  [local(): return (mine + jnp.sum(others.astype(F32), axis=0)).astype(BF16)]
    unnamed x1 -> x0, local copies, waits for them, and re-layouts: 1.67 us -> none
    pallas_call x1, Pallas kernels: 27.9 us -> 27.3 us  [local(): pl.pallas_call(functools.partial(kernel, reach, n_ctx, n_tp, docs), out_s...]
where the time goes in v3:
time: 29.3 us; the launch traced here: 29.2 us
  Pallas kernels  27.3 us (93%)
  other arithmetic  1.88 us (6%)
    pallas_call x1, Pallas kernels, local(): pl.pallas_call(functools.partial(kernel, reach, n_ctx, n_tp, docs), out_s...  27.3 us
    convert_element_type x1, other arithmetic, local(): return (mine + jnp.sum(others.astype(F32), axis=0)).astype(BF16)  1.88 us

profile of v3, /device:TPU:16, one launch (start us, length us, event | category | flops | bytes accessed | tf_op | source)
XLA Modules:
  0.0 29.2 jit_solution(12126567058749283131)
XLA Ops:
  0.0 27.3 %attention_layer.1 = (f32[256,512]{1,0:T(8,128)}, bf16[1,256,512]{2,1,0:T(8,128)(2,1)}) custom-call(s32[16]{0:T(128)} %docs_hbm.1, bf16[256,2048]{1,0:T(8,128)(2,1)} %tok_hbm.1, bf16[2048,1024]{1,0:T(8,128)(2,1)} %wq_hbm.1, bf16[2048,512]{1,0:T(8,128)(2,1)} %wk_hbm.1, bf16[2048,512]{1,0:T(8,128)(2,1)} %wv_hbm.1, bf16[1024,2048]{1,0:T(8,128)(2,1)} %wo_hbm.1, ...), custom_call_target="tpu_custom_call" | custom-call | flops 5100273664 | bytes 10485760 | tf_op jit(solution)/shard_map/attention_layer/pallas_call | solution.py:388
  27.3 1.9 %fusion = bf16[256,512]{1,0:T(8,128)(2,1)} fusion(f32[256,512]{1,0:T(8,128)} %get-tuple-element.7, bf16[1,256,512]{2,1,0:T(8,128)(2,1)} %get-tuple-element.8), kind=kLoop, calls=%fused_computation.1 | loop fusion | flops 393216 | bytes 1048576 | tf_op jit(solution)/shard_map/convert_element_type | solution.py:441

commit v4 on v3

--- a/solution.py
+++ b/solution.py
@@ -89,14 +89,13 @@
         first.append(fetch(wk_hbm.at[deep, kv_cols], wkv.at[deep, pl.ds(0, HD)], tok_sem.at[1, n]))
         first.append(fetch(wv_hbm.at[deep, kv_cols], wkv.at[deep, pl.ds(HD, HD)], tok_sem.at[2, n]))
     q_parts = heads // 2
-    wq_copies = [
-        fetch(
-            wq_hbm.at[:, pl.ds(n * 2 * HD, 2 * HD)],
-            wq.at[:, pl.ds(n * 2 * HD, 2 * HD)],
-            wq_sem.at[n],
-        )
-        for n in range(q_parts)
-    ]
+
+    def wq_copy(n):
+        cols = pl.ds(pl.multiple_of(n * 2 * HD, 2 * HD), 2 * HD)
+        return pltpu.make_async_copy(wq_hbm.at[:, cols], wq.at[:, cols], wq_sem.at[n])
+
+    for n in range(q_parts):
+        wq_copy(n).start()
 
     barrier = pltpu.get_barrier_semaphore()
 
@@ -159,7 +158,7 @@
     part = rows // PIECES
 
     def hop(src, dst, piece, where, sems):
-        here = (slice(None), pl.ds(piece * part, part), slice(None))
+        here = (slice(None), pl.ds(pl.multiple_of(piece * part, part), part), slice(None))
         return pltpu.make_async_remote_copy(
             src_ref=kv.at[(src,) + here],
             dst_ref=kv.at[(dst,) + here],
@@ -231,17 +230,18 @@
                 q_s[c, pl.ds(at, ct), pl.ds(0, HD)] = one[c * ct : (c + 1) * ct]
         return 0
 
-    early = q_parts - 2
-    for n in range(early):
-        wq_copies[n].wait()
-    lax.fori_loop(0, early, project, 0)
-    forward(2, every[:1])
-    wq_copies[early].wait()
-    project(early, 0)
-    forward(2, every[1:2])
-    wq_copies[early + 1].wait()
-    project(early + 1, 0)
-    forward(2, every[2:])
+    def query_part(n, _):
+        wq_copy(n).wait()
+        project(n, 0)
+
+        @pl.when(n >= 1)
+        def _():
+            forward(2, [n - 1])
+
+        return 0
+
+    lax.fori_loop(0, q_parts, query_part, 0)
+    forward(2, every[q_parts - 1 :])
 
     group = min(8, heads)
     grows = group * ct
@@ -310,7 +310,7 @@
     def chip_copy(c, k):
         return pltpu.make_async_remote_copy(
             src_ref=s2.at[c, k - 1],
-            dst_ref=r2.at[k - 1, pl.ds(c * ct, ct)],
+            dst_ref=r2.at[k - 1, pl.ds(pl.multiple_of(c * ct, ct), ct)],
             send_sem=s2_send.at[c, k - 1],
             recv_sem=s2_recv.at[c, k - 1],
             device_id=(i, (t + 2 * k) % n_tp),
@@ -318,38 +318,59 @@
         )
 
     def kept(c):
-        return pltpu.make_async_copy(own.at[c], mine_ref.at[pl.ds(c * ct, ct)], own_sem.at[c])
+        return pltpu.make_async_copy(
+            own.at[c, 0], mine_ref.at[pl.ds(pl.multiple_of(c * ct, ct), ct)], own_sem.at[c]
+        )
 
     def columns(owner):
         return pl.ds(pl.multiple_of(owner * cw, cw), cw)
 
-    for c in range(chunks):
-
-        def finish(n, _):
+    def finish(c):
+        def step(n, _):
             at = pl.multiple_of(n * grows, grows)
             total = acc[c, pl.ds(at, grows), :]
             total = total + weighted(c, at, reach) + weighted(c, at, reach - 1)
             done = (total[:, :HD] / total[:, HD:]).astype(BF16)
             for h in range(group):
                 cols = pl.ds(pl.multiple_of(n * group * HD + h * HD, HD), HD)
-                att[c, :, cols] = done[h * ct : (h + 1) * ct]
+                att[:, cols] = done[h * ct : (h + 1) * ct]
             return 0
 
-        lax.fori_loop(0, groups, finish, 0)
-        order = list(range(1, nb)) + [0]
+        if groups == 1:
+            step(0, 0)
+        else:
+            lax.fori_loop(0, groups, step, 0)
+
+    order = list(range(1, nb)) + [0]
+
+    def pair_sum(c):
         for k in order:
-            s1[c, k] = mm(att[c], wo[:, columns((partner + 2 * k) % n_tp)]).astype(BF16)
-            pair_copy(c, k).start()
-        for k in order:
-            term = mm(att[c], wo[:, columns((t + 2 * k) % n_tp)]).astype(BF16).astype(F32)
             pair_copy(c, k).wait_recv()
-            term = term + r1[c, k].astype(F32)
+            term = own[c, k] + r1[c, k].astype(F32)
             if k:
                 s2[c, k - 1] = term.astype(BF16)
                 chip_copy(c, k).start()
             else:
-                own[c] = term
+                own[c, 0] = term
                 kept(c).start()
+
+    def chunk(c, _):
+        finish(c)
+
+        @pl.when(c >= 1)
+        def _():
+            pair_sum(c - 1)
+
+        for k in order:
+            s1[c, k] = mm(att[...], wo[:, columns((partner + 2 * k) % n_tp)]).astype(BF16)
+            pair_copy(c, k).start()
+        for k in order:
+            term = mm(att[...], wo[:, columns((t + 2 * k) % n_tp)])
+            own[c, k] = term.astype(BF16).astype(F32)
+        return 0
+
+    lax.fori_loop(0, chunks, chunk, 0)
+    pair_sum(chunks - 1)
 
     for c in range(chunks):
         kept(c).wait()
@@ -408,11 +429,11 @@
             pltpu.VMEM((reach + 1, HD + wide, rows), BF16),
             pltpu.VMEM((chunks, heads * ct, HD + wide), BF16),
             pltpu.VMEM((chunks, heads * ct, 2 * HD), F32),
-            pltpu.VMEM((chunks, ct, heads * HD), BF16),
+            pltpu.VMEM((ct, heads * HD), BF16),
             pltpu.VMEM((chunks, nb, ct, cw), BF16),
             pltpu.VMEM((chunks, nb, ct, cw), BF16),
             pltpu.VMEM((chunks, nb - 1, ct, cw), BF16),
-            pltpu.VMEM((chunks, ct, cw), F32),
+            pltpu.VMEM((chunks, nb, ct, cw), F32),
             dma((4 + LOADS,)),
             dma((3, LOADS)),
             dma((heads // 2,)),

time: 29.3 us -> 28.6 us (0.976)
  Pallas kernels: 27.3 us -> 26.5 us
    pallas_call x1, Pallas kernels: 27.3 us -> 26.5 us  [local(): pl.pallas_call(functools.partial(kernel, reach, n_ctx, n_tp, docs), out_s...]
where the time goes in v4:
time: 28.6 us; the launch traced here: 28.4 us
  Pallas kernels  26.5 us (93%)
  other arithmetic  1.88 us (7%)
    pallas_call x1, Pallas kernels, local(): pl.pallas_call(functools.partial(kernel, reach, n_ctx, n_tp, docs), out_s...  26.5 us
    convert_element_type x1, other arithmetic, local(): return (mine + jnp.sum(others.astype(F32), axis=0)).astype(BF16)  1.88 us

profile of v4, /device:TPU:16, one launch (start us, length us, event | category | flops | bytes accessed | tf_op | source)
XLA Modules:
  0.0 28.4 jit_solution(8921705536184392513)
XLA Ops:
  0.0 26.5 %attention_layer.1 = (f32[256,512]{1,0:T(8,128)}, bf16[1,256,512]{2,1,0:T(8,128)(2,1)}) custom-call(s32[16]{0:T(128)} %docs_hbm.1, bf16[256,2048]{1,0:T(8,128)(2,1)} %tok_hbm.1, bf16[2048,1024]{1,0:T(8,128)(2,1)} %wq_hbm.1, bf16[2048,512]{1,0:T(8,128)(2,1)} %wk_hbm.1, bf16[2048,512]{1,0:T(8,128)(2,1)} %wv_hbm.1, bf16[1024,2048]{1,0:T(8,128)(2,1)} %wo_hbm.1, ...), custom_call_target="tpu_custom_call" | custom-call | flops 5100273664 | bytes 10485760 | tf_op jit(solution)/shard_map/attention_layer/pallas_call | solution.py:409
  26.5 1.9 %fusion = bf16[256,512]{1,0:T(8,128)(2,1)} fusion(f32[256,512]{1,0:T(8,128)} %get-tuple-element.7, bf16[1,256,512]{2,1,0:T(8,128)(2,1)} %get-tuple-element.8), kind=kLoop, calls=%fused_computation.1 | loop fusion | flops 393216 | bytes 1048576 | tf_op jit(solution)/shard_map/convert_element_type | solution.py:462

commit v5 on v4

--- a/solution.py
+++ b/solution.py
@@ -52,7 +52,7 @@
     reach, n_ctx, n_tp, docs,
     docs_hbm, tok_hbm, wq_hbm, wk_hbm, wv_hbm, wo_hbm, qg_hbm, kg_hbm, fr_hbm,
     mine_ref, r2,
-    docs_ref, tok, wkv, wq, wo, qg, kg, fr, cos2, sin2, kv, kt, q_s, acc, att, s1, r1, s2, own,
+    docs_ref, tok, wkv, wq, wo, qg, kg, fr, cos2, sin2, kv, kt, vt, q_s, acc, att, s1, r1, s2, s1_own, r1_own, own,
     in_sem, tok_sem, wq_sem, own_sem, z_send, y_send, kv_recv, s1_send, s1_recv, s2_send, s2_recv,
 ):
     rows = tok.shape[0]
@@ -131,6 +131,11 @@
     local = lax.broadcasted_iota(jnp.int32, (rows, wide), 0)
     lanes = lax.broadcasted_iota(jnp.int32, (rows, wide), 1)
 
+    def nth(j):
+        if j == 0:
+            return 0
+        return j + (1 - i % 2) * (1 if j % 2 else -1)
+
     def members(d):
         pos = local + (i - d) * rows
         return (pos >= starts) & (pos < ends)
@@ -205,7 +210,8 @@
     ]
 
     for d in range(reach + 1):
-        held = jnp.where(members(d), HIDE, jnp.where(lanes == docs, -HIDE, 0.0))
+        vt[d, :, pl.ds(HD, HD)] = jnp.ones((rows, HD), BF16)
+        held = jnp.where(members(nth(d)), HIDE, jnp.where(lanes == docs, -HIDE, 0.0))
         kt[d, pl.ds(HD, wide), :] = held.T.astype(BF16)
     q_code = jnp.where(mine | (lanes == docs), 1.0, 0.0).astype(BF16)
     for c in range(chunks):
@@ -246,31 +252,51 @@
     group = min(8, heads)
     grows = group * ct
     groups = heads // group
-    ones = jnp.ones((rows, HD), BF16)
-
-    def weights_of(c, at, d):
+
+    def weights_of(c, at, d, first):
         weights = jnp.exp2(mm(q_s[c, pl.ds(at, grows), :], kt[d]))
-        if d == 0:
+        if first:
             token = lax.broadcasted_iota(jnp.int32, (ct, rows), 0) + c * ct
             seen = lax.broadcasted_iota(jnp.int32, (ct, rows), 1) <= token
             weights = jnp.where(seen[None], weights.reshape(group, ct, rows), 0.0)
             weights = weights.reshape(grows, rows)
         return weights.astype(BF16)
 
-    def weighted(c, at, d):
-        return mm(weights_of(c, at, d), jnp.concatenate([kv[d, 1], ones], axis=1))
-
-    def turn(d):
-        kt[d, pl.ds(0, HD), :] = kv[d, 0].astype(F32).T.astype(BF16)
-
-    def attend(d):
+    def weighted(c, at, d, first=False):
+        return mm(weights_of(c, at, d, first), vt[d])
+
+    def place(j, d):
+        if d % 2:
+
+            @pl.when(i >= d)
+            def _():
+                for piece in every:
+                    hop(0, d, piece, pair, z_send).wait_recv()
+
+        kt[j, pl.ds(0, HD), :] = kv[d, 0].astype(F32).T.astype(BF16)
+        vt[j, :, pl.ds(0, HD)] = kv[d, 1]
+
+    def turn(j):
+        if j == 0:
+            place(0, 0)
+            return
+
+        @pl.when(odd)
+        def _():
+            place(j, j)
+
+        @pl.when(jnp.logical_not(odd))
+        def _():
+            place(j, j + 1 if j % 2 else j - 1)
+
+    def attend(d, first=False):
         turn(d)
 
         def step(n, _):
             c = n // groups
             at = pl.multiple_of((n % groups) * grows, grows)
-            new = weighted(c, at, d)
-            if d == 0:
+            new = weighted(c, at, d, first)
+            if first:
                 acc[c, pl.ds(at, grows), :] = new
             else:
                 acc[c, pl.ds(at, grows), :] += new
@@ -279,28 +305,24 @@
         lax.fori_loop(0, chunks * groups, step, 0)
 
     forward(4, every[:1])
-    attend(0)
+    attend(0, True)
     forward(4, every[1:])
-    attend(2)
-    for d in range(6, reach + 1, 2):
-        forward(d, every)
-        attend(d - 2)
-    for d in range(1, reach - 1, 2):
-        for piece in every:
-            arrive(d, piece)
-        attend(d)
+    for j in range(1, reach):
+        if j > 2 and j % 2 and j + 3 <= reach:
+            forward(j + 3, every)
+        attend(j)
     turn(reach)
-    for piece in every:
-        arrive(reach - 1, piece)
-    turn(reach - 1)
 
     for copy in wo_copies:
         copy.wait()
 
+    def some_rows(c):
+        return pl.ds(pl.multiple_of(c * ct, ct), ct)
+
     def pair_copy(c, k):
         return pltpu.make_async_remote_copy(
-            src_ref=s1.at[c, k],
-            dst_ref=r1.at[c, k],
+            src_ref=s1.at[c, k - 1],
+            dst_ref=r1.at[c, k - 1],
             send_sem=s1_send.at[c, k],
             recv_sem=s1_recv.at[c, k],
             device_id=(i, partner),
@@ -310,17 +332,22 @@
     def chip_copy(c, k):
         return pltpu.make_async_remote_copy(
             src_ref=s2.at[c, k - 1],
-            dst_ref=r2.at[k - 1, pl.ds(pl.multiple_of(c * ct, ct), ct)],
+            dst_ref=r2.at[k - 1, some_rows(c)],
             send_sem=s2_send.at[c, k - 1],
             recv_sem=s2_recv.at[c, k - 1],
             device_id=(i, (t + 2 * k) % n_tp),
             device_id_type=MESH,
         )
 
-    def kept(c):
-        return pltpu.make_async_copy(
-            own.at[c, 0], mine_ref.at[pl.ds(pl.multiple_of(c * ct, ct), ct)], own_sem.at[c]
-        )
+    own_copy = pltpu.make_async_remote_copy(
+        src_ref=s1_own,
+        dst_ref=r1_own,
+        send_sem=s1_send.at[0, 0],
+        recv_sem=s1_recv.at[0, 0],
+        device_id=(i, partner),
+        device_id_type=MESH,
+    )
+    kept = pltpu.make_async_copy(own.at[0], mine_ref, own_sem.at[0])
 
     def columns(owner):
         return pl.ds(pl.multiple_of(owner * cw, cw), cw)
@@ -328,12 +355,11 @@
     def finish(c):
         def step(n, _):
             at = pl.multiple_of(n * grows, grows)
-            total = acc[c, pl.ds(at, grows), :]
-            total = total + weighted(c, at, reach) + weighted(c, at, reach - 1)
+            total = acc[c, pl.ds(at, grows), :] + weighted(c, at, reach)
             done = (total[:, :HD] / total[:, HD:]).astype(BF16)
             for h in range(group):
                 cols = pl.ds(pl.multiple_of(n * group * HD + h * HD, HD), HD)
-                att[:, cols] = done[h * ct : (h + 1) * ct]
+                att[some_rows(c), cols] = done[h * ct : (h + 1) * ct]
             return 0
 
         if groups == 1:
@@ -341,18 +367,12 @@
         else:
             lax.fori_loop(0, groups, step, 0)
 
-    order = list(range(1, nb)) + [0]
-
     def pair_sum(c):
-        for k in order:
+        for k in range(1, nb):
             pair_copy(c, k).wait_recv()
-            term = own[c, k] + r1[c, k].astype(F32)
-            if k:
-                s2[c, k - 1] = term.astype(BF16)
-                chip_copy(c, k).start()
-            else:
-                own[c, 0] = term
-                kept(c).start()
+            term = own[k, some_rows(c)] + r1[c, k - 1].astype(F32)
+            s2[c, k - 1] = term.astype(BF16)
+            chip_copy(c, k).start()
 
     def chunk(c, _):
         finish(c)
@@ -361,27 +381,33 @@
         def _():
             pair_sum(c - 1)
 
-        for k in order:
-            s1[c, k] = mm(att[...], wo[:, columns((partner + 2 * k) % n_tp)]).astype(BF16)
+        for k in range(1, nb):
+            term = mm(att[some_rows(c)], wo[:, columns((partner + 2 * k) % n_tp)])
+            s1[c, k - 1] = term.astype(BF16)
             pair_copy(c, k).start()
-        for k in order:
-            term = mm(att[...], wo[:, columns((t + 2 * k) % n_tp)])
-            own[c, k] = term.astype(BF16).astype(F32)
+        for k in range(1, nb):
+            term = mm(att[some_rows(c)], wo[:, columns((t + 2 * k) % n_tp)])
+            own[k, some_rows(c)] = term.astype(BF16).astype(F32)
         return 0
 
     lax.fori_loop(0, chunks, chunk, 0)
     pair_sum(chunks - 1)
-
+    s1_own[...] = mm(att[...], wo[:, columns(partner)]).astype(BF16)
+    own_copy.start()
+    own[0] = mm(att[...], wo[:, columns(t)]).astype(BF16).astype(F32)
+    own_copy.wait_recv()
+    own[0] += r1_own[...].astype(F32)
+    kept.start()
+    kept.wait()
     for c in range(chunks):
-        kept(c).wait()
         for k in range(1, nb):
             chip_copy(c, k).wait_recv()
 
+    own_copy.wait_send()
     for c in range(chunks):
-        for k in range(nb):
+        for k in range(1, nb):
             pair_copy(c, k).wait_send()
-            if k:
-                chip_copy(c, k).wait_send()
+            chip_copy(c, k).wait_send()
     for d in range(0, reach + 1, 2):
         for piece in every:
             for cond, copy in hops(d, piece):
@@ -427,13 +453,16 @@
             pltpu.VMEM((rows, HD), F32),
             pltpu.VMEM((reach + 1, 2, rows, HD), BF16),
             pltpu.VMEM((reach + 1, HD + wide, rows), BF16),
+            pltpu.VMEM((reach + 1, rows, 2 * HD), BF16),
             pltpu.VMEM((chunks, heads * ct, HD + wide), BF16),
             pltpu.VMEM((chunks, heads * ct, 2 * HD), F32),
-            pltpu.VMEM((ct, heads * HD), BF16),
-            pltpu.VMEM((chunks, nb, ct, cw), BF16),
-            pltpu.VMEM((chunks, nb, ct, cw), BF16),
+            pltpu.VMEM((rows, heads * HD), BF16),
             pltpu.VMEM((chunks, nb - 1, ct, cw), BF16),
-            pltpu.VMEM((chunks, nb, ct, cw), F32),
+            pltpu.VMEM((chunks, nb - 1, ct, cw), BF16),
+            pltpu.VMEM((chunks, nb - 1, ct, cw), BF16),
+            pltpu.VMEM((rows, cw), BF16),
+            pltpu.VMEM((rows, cw), BF16),
+            pltpu.VMEM((nb, rows, cw), F32),
             dma((4 + LOADS,)),
             dma((3, LOADS)),
             dma((heads // 2,)),

time: 28.6 us -> 28.8 us (level)
  no operation moved by 1% of the time
where the time goes in v5:
time: 28.8 us; the launch traced here: 28.6 us
  Pallas kernels  26.7 us (93%)
  other arithmetic  1.88 us (7%)
    pallas_call x1, Pallas kernels, local(): pl.pallas_call(functools.partial(kernel, reach, n_ctx, n_tp, docs), out_s...  26.7 us
    convert_element_type x1, other arithmetic, local(): return (mine + jnp.sum(others.astype(F32), axis=0)).astype(BF16)  1.88 us

profile of v5, /device:TPU:16, one launch (start us, length us, event | category | flops | bytes accessed | tf_op | source)
XLA Modules:
  0.0 28.6 jit_solution(18263324194065704913)
XLA Ops:
  0.0 26.7 %attention_layer.1 = (f32[256,512]{1,0:T(8,128)}, bf16[1,256,512]{2,1,0:T(8,128)(2,1)}) custom-call(s32[16]{0:T(128)} %docs_hbm.1, bf16[256,2048]{1,0:T(8,128)(2,1)} %tok_hbm.1, bf16[2048,1024]{1,0:T(8,128)(2,1)} %wq_hbm.1, bf16[2048,512]{1,0:T(8,128)(2,1)} %wk_hbm.1, bf16[2048,512]{1,0:T(8,128)(2,1)} %wv_hbm.1, bf16[1024,2048]{1,0:T(8,128)(2,1)} %wo_hbm.1, ...), custom_call_target="tpu_custom_call" | custom-call | flops 5100273664 | bytes 10485760 | tf_op jit(solution)/shard_map/attention_layer/pallas_call | solution.py:435
  26.7 1.9 %fusion = bf16[256,512]{1,0:T(8,128)(2,1)} fusion(f32[256,512]{1,0:T(8,128)} %get-tuple-element.7, bf16[1,256,512]{2,1,0:T(8,128)(2,1)} %get-tuple-element.8), kind=kLoop, calls=%fused_computation.1 | loop fusion | flops 393216 | bytes 1048576 | tf_op jit(solution)/shard_map/convert_element_type | solution.py:491

commit v6 on v5

--- a/solution.py
+++ b/solution.py
@@ -16,7 +16,7 @@
 ROPE_BASE = 1000000.0
 HIDE = 256.0
 CHUNKS = 4
-PIECES = 4
+PIECES = 2
 LOADS = 4
 MESH = pl.DeviceIdType.MESH
 BF16 = jnp.bfloat16
@@ -94,9 +94,6 @@
         cols = pl.ds(pl.multiple_of(n * 2 * HD, 2 * HD), 2 * HD)
         return pltpu.make_async_copy(wq_hbm.at[:, cols], wq.at[:, cols], wq_sem.at[n])
 
-    for n in range(q_parts):
-        wq_copy(n).start()
-
     barrier = pltpu.get_barrier_semaphore()
 
     def greet(where):
@@ -153,6 +150,8 @@
 
     for copy in first:
         copy.wait()
+    for n in range(q_parts):
+        wq_copy(n).start()
     projected = mm(tok[...], wkv[...])
     kv[0, 0] = norm_rotate(projected[:, :HD], kg[...], cos2[...], sin2[...]).astype(BF16)
     kv[0, 1] = projected[:, HD:].astype(BF16)
@@ -240,30 +239,31 @@
         wq_copy(n).wait()
         project(n, 0)
 
-        @pl.when(n >= 1)
+        @pl.when(n >= q_parts - PIECES + 1)
         def _():
-            forward(2, [n - 1])
+            forward(2, [n - (q_parts - PIECES + 1)])
 
         return 0
 
     lax.fori_loop(0, q_parts, query_part, 0)
-    forward(2, every[q_parts - 1 :])
+    forward(2, every[PIECES - 1 :])
 
     group = min(8, heads)
     grows = group * ct
     groups = heads // group
 
-    def weights_of(c, at, d, first):
-        weights = jnp.exp2(mm(q_s[c, pl.ds(at, grows), :], kt[d]))
-        if first:
+    def weights_of(c, at, j):
+        weights = jnp.exp2(mm(q_s[c, pl.ds(at, grows), :], kt[j]))
+        if j == 0:
             token = lax.broadcasted_iota(jnp.int32, (ct, rows), 0) + c * ct
             seen = lax.broadcasted_iota(jnp.int32, (ct, rows), 1) <= token
             weights = jnp.where(seen[None], weights.reshape(group, ct, rows), 0.0)
             weights = weights.reshape(grows, rows)
         return weights.astype(BF16)
 
-    def weighted(c, at, d, first=False):
-        return mm(weights_of(c, at, d, first), vt[d])
+    def weighted(c, at, slots):
+        weights = jnp.concatenate([weights_of(c, at, j) for j in slots], axis=1)
+        return mm(weights, jnp.concatenate([vt[j] for j in slots], axis=0))
 
     def place(j, d):
         if d % 2:
@@ -289,14 +289,15 @@
         def _():
             place(j, j + 1 if j % 2 else j - 1)
 
-    def attend(d, first=False):
-        turn(d)
+    def attend(slots):
+        for j in slots:
+            turn(j)
 
         def step(n, _):
             c = n // groups
             at = pl.multiple_of((n % groups) * grows, grows)
-            new = weighted(c, at, d, first)
-            if first:
+            new = weighted(c, at, slots)
+            if slots[0] == 0:
                 acc[c, pl.ds(at, grows), :] = new
             else:
                 acc[c, pl.ds(at, grows), :] += new
@@ -305,12 +306,12 @@
         lax.fori_loop(0, chunks * groups, step, 0)
 
     forward(4, every[:1])
-    attend(0, True)
+    attend((0, 1))
     forward(4, every[1:])
-    for j in range(1, reach):
-        if j > 2 and j % 2 and j + 3 <= reach:
-            forward(j + 3, every)
-        attend(j)
+    for j in range(2, reach, 2):
+        if j > 2:
+            forward(j + 2, every)
+        attend((j, j + 1))
     turn(reach)
 
     for copy in wo_copies:
@@ -355,7 +356,7 @@
     def finish(c):
         def step(n, _):
             at = pl.multiple_of(n * grows, grows)
-            total = acc[c, pl.ds(at, grows), :] + weighted(c, at, reach)
+            total = acc[c, pl.ds(at, grows), :] + weighted(c, at, (reach,))
             done = (total[:, :HD] / total[:, HD:]).astype(BF16)
             for h in range(group):
                 cols = pl.ds(pl.multiple_of(n * group * HD + h * HD, HD), HD)
@@ -398,12 +399,8 @@
     own_copy.wait_recv()
     own[0] += r1_own[...].astype(F32)
     kept.start()
+    own_copy.wait_send()
     kept.wait()
-    for c in range(chunks):
-        for k in range(1, nb):
-            chip_copy(c, k).wait_recv()
-
-    own_copy.wait_send()
     for c in range(chunks):
         for k in range(1, nb):
             pair_copy(c, k).wait_send()
@@ -415,6 +412,9 @@
                 @pl.when(cond)
                 def _():
                     copy.wait_send()
+    for c in range(chunks):
+        for k in range(1, nb):
+            chip_copy(c, k).wait_recv()
 
 
 def local(n_ctx, n_tp, tokens, w_query, w_key, w_value, w_out, query_gain, key_gain, doc_lengths):

time: 28.8 us -> 27.8 us (0.965)
  Pallas kernels: 26.7 us -> 25.6 us
    pallas_call x1, Pallas kernels: 26.7 us -> 25.6 us  [local(): pl.pallas_call(functools.partial(kernel, reach, n_ctx, n_tp, docs), out_s...]
where the time goes in v6:
time: 27.8 us; the launch traced here: 27.5 us
  Pallas kernels  25.6 us (92%)
  other arithmetic  1.88 us (7%)
    pallas_call x1, Pallas kernels, local(): pl.pallas_call(functools.partial(kernel, reach, n_ctx, n_tp, docs), out_s...  25.6 us
    convert_element_type x1, other arithmetic, local(): return (mine + jnp.sum(others.astype(F32), axis=0)).astype(BF16)  1.88 us

profile of v6, /device:TPU:16, one launch (start us, length us, event | category | flops | bytes accessed | tf_op | source)
XLA Modules:
  0.0 27.5 jit_solution(349984838087876314)
XLA Ops:
  0.0 25.6 %attention_layer.1 = (f32[256,512]{1,0:T(8,128)}, bf16[1,256,512]{2,1,0:T(8,128)(2,1)}) custom-call(s32[16]{0:T(128)} %docs_hbm.1, bf16[256,2048]{1,0:T(8,128)(2,1)} %tok_hbm.1, bf16[2048,1024]{1,0:T(8,128)(2,1)} %wq_hbm.1, bf16[2048,512]{1,0:T(8,128)(2,1)} %wk_hbm.1, bf16[2048,512]{1,0:T(8,128)(2,1)} %wv_hbm.1, bf16[1024,2048]{1,0:T(8,128)(2,1)} %wo_hbm.1, ...), custom_call_target="tpu_custom_call" | custom-call | flops 5100273664 | bytes 10485760 | tf_op jit(solution)/shard_map/attention_layer/pallas_call | solution.py:435
  25.6 1.9 %fusion = bf16[256,512]{1,0:T(8,128)(2,1)} fusion(f32[256,512]{1,0:T(8,128)} %get-tuple-element.7, bf16[1,256,512]{2,1,0:T(8,128)(2,1)} %get-tuple-element.8), kind=kLoop, calls=%fused_computation.1 | loop fusion | flops 393216 | bytes 1048576 | tf_op jit(solution)/shard_map/convert_element_type | solution.py:491

commit v7 on v6

--- a/solution.py
+++ b/solution.py
@@ -16,7 +16,7 @@
 ROPE_BASE = 1000000.0
 HIDE = 256.0
 CHUNKS = 4
-PIECES = 2
+PIECES = 4
 LOADS = 4
 MESH = pl.DeviceIdType.MESH
 BF16 = jnp.bfloat16
@@ -239,14 +239,14 @@
         wq_copy(n).wait()
         project(n, 0)
 
-        @pl.when(n >= q_parts - PIECES + 1)
-        def _():
-            forward(2, [n - (q_parts - PIECES + 1)])
+        @pl.when(n >= 1)
+        def _():
+            forward(2, [n - 1])
 
         return 0
 
     lax.fori_loop(0, q_parts, query_part, 0)
-    forward(2, every[PIECES - 1 :])
+    forward(2, every[q_parts - 1 :])
 
     group = min(8, heads)
     grows = group * ct
@@ -289,7 +289,7 @@
         def _():
             place(j, j + 1 if j % 2 else j - 1)
 
-    def attend(slots):
+    def attend(slots, between=None):
         for j in slots:
             turn(j)
 
@@ -301,13 +301,21 @@
                 acc[c, pl.ds(at, grows), :] = new
             else:
                 acc[c, pl.ds(at, grows), :] += new
+            if between is not None:
+                between(n)
             return 0
 
         lax.fori_loop(0, chunks * groups, step, 0)
 
-    forward(4, every[:1])
-    attend((0, 1))
-    forward(4, every[1:])
+    steps = chunks * groups
+
+    def second_hop(n):
+        @pl.when(n < PIECES)
+        def _():
+            forward(4, [n])
+
+    attend((0, 1), second_hop)
+    forward(4, every[steps:])
     for j in range(2, reach, 2):
         if j > 2:
             forward(j + 2, every)

time: 27.8 us -> 26.3 us (0.946)
  Pallas kernels: 25.6 us -> 24.2 us
    pallas_call x1, Pallas kernels: 25.6 us -> 24.2 us  [local(): pl.pallas_call(functools.partial(kernel, reach, n_ctx, n_tp, docs), out_s...]
where the time goes in v7:
time: 26.3 us; the launch traced here: 26.1 us
  Pallas kernels  24.2 us (92%)
  other arithmetic  1.88 us (7%)
    pallas_call x1, Pallas kernels, local(): pl.pallas_call(functools.partial(kernel, reach, n_ctx, n_tp, docs), out_s...  24.2 us
    convert_element_type x1, other arithmetic, local(): return (mine + jnp.sum(others.astype(F32), axis=0)).astype(BF16)  1.88 us

profile of v7, /device:TPU:16, one launch (start us, length us, event | category | flops | bytes accessed | tf_op | source)
XLA Modules:
  0.0 26.1 jit_solution(15823274705887980561)
XLA Ops:
  0.0 24.2 %attention_layer.1 = (f32[256,512]{1,0:T(8,128)}, bf16[1,256,512]{2,1,0:T(8,128)(2,1)}) custom-call(s32[16]{0:T(128)} %docs_hbm.1, bf16[256,2048]{1,0:T(8,128)(2,1)} %tok_hbm.1, bf16[2048,1024]{1,0:T(8,128)(2,1)} %wq_hbm.1, bf16[2048,512]{1,0:T(8,128)(2,1)} %wk_hbm.1, bf16[2048,512]{1,0:T(8,128)(2,1)} %wv_hbm.1, bf16[1024,2048]{1,0:T(8,128)(2,1)} %wo_hbm.1, ...), custom_call_target="tpu_custom_call" | custom-call | flops 5100273664 | bytes 10485760 | tf_op jit(solution)/shard_map/attention_layer/pallas_call | solution.py:443
  24.2 1.9 %fusion = bf16[256,512]{1,0:T(8,128)(2,1)} fusion(f32[256,512]{1,0:T(8,128)} %get-tuple-element.7, bf16[1,256,512]{2,1,0:T(8,128)(2,1)} %get-tuple-element.8), kind=kLoop, calls=%fused_computation.1 | loop fusion | flops 393216 | bytes 1048576 | tf_op jit(solution)/shard_map/convert_element_type | solution.py:499

commit v8 on v7

--- a/solution.py
+++ b/solution.py
@@ -208,20 +208,6 @@
         for n in range(LOADS)
     ]
 
-    for d in range(reach + 1):
-        vt[d, :, pl.ds(HD, HD)] = jnp.ones((rows, HD), BF16)
-        held = jnp.where(members(nth(d)), HIDE, jnp.where(lanes == docs, -HIDE, 0.0))
-        kt[d, pl.ds(HD, wide), :] = held.T.astype(BF16)
-    q_code = jnp.where(mine | (lanes == docs), 1.0, 0.0).astype(BF16)
-    for c in range(chunks):
-        for h in range(heads):
-            q_s[c, pl.ds(h * ct, ct), pl.ds(HD, wide)] = q_code[c * ct : (c + 1) * ct]
-    for d in range(1, reach + 1):
-
-        @pl.when(i < d)
-        def _():
-            kv[d] = jnp.zeros(kv.shape[1:], BF16)
-
     scale = HD ** (-0.5) * math.log2(math.e)
 
     def project(n, _):
@@ -246,6 +232,33 @@
         return 0
 
     lax.fori_loop(0, q_parts, query_part, 0)
+    across = (HD, wide)
+    starts_down = jnp.broadcast_to(starts.astype(F32), across).T
+    ends_down = jnp.broadcast_to(ends.astype(F32), across).T
+    starts_down = jnp.concatenate([starts_down] * (rows // HD), axis=1)
+    ends_down = jnp.concatenate([ends_down] * (rows // HD), axis=1)
+    key_at = lax.broadcasted_iota(jnp.int32, (wide, rows), 1)
+    doc_at = lax.broadcasted_iota(jnp.int32, (wide, rows), 0)
+
+    def key_codes(slots):
+        for j in slots:
+            vt[j, :, pl.ds(HD, HD)] = jnp.ones((rows, HD), BF16)
+            place_of = (key_at + (i - nth(j)) * rows).astype(F32)
+            member = (place_of >= starts_down) & (place_of < ends_down)
+            held = jnp.where(member, HIDE, jnp.where(doc_at == docs, -HIDE, 0.0))
+            kt[j, pl.ds(HD, wide), :] = held.astype(BF16)
+
+    key_codes((0, 1))
+    q_code = jnp.where(mine | (lanes == docs), 1.0, 0.0).astype(BF16)
+    for c in range(chunks):
+        for h in range(heads):
+            q_s[c, pl.ds(h * ct, ct), pl.ds(HD, wide)] = q_code[c * ct : (c + 1) * ct]
+    for d in range(1, reach + 1):
+
+        @pl.when(i < d)
+        def _():
+            kv[d] = jnp.zeros(kv.shape[1:], BF16)
+
     forward(2, every[q_parts - 1 :])
 
     group = min(8, heads)
@@ -316,6 +329,7 @@
 
     attend((0, 1), second_hop)
     forward(4, every[steps:])
+    key_codes(range(2, reach + 1))
     for j in range(2, reach, 2):
         if j > 2:
             forward(j + 2, every)

time: 26.3 us -> 26.3 us (level)
  no operation moved by 1% of the time
where the time goes in v8:
time: 26.3 us; the launch traced here: 26.1 us
  Pallas kernels  24.2 us (92%)
  other arithmetic  1.88 us (7%)
    pallas_call x1, Pallas kernels, local(): pl.pallas_call(functools.partial(kernel, reach, n_ctx, n_tp, docs), out_s...  24.2 us
    convert_element_type x1, other arithmetic, local(): return (mine + jnp.sum(others.astype(F32), axis=0)).astype(BF16)  1.88 us

profile of v8, /device:TPU:16, one launch (start us, length us, event | category | flops | bytes accessed | tf_op | source)
XLA Modules:
  0.0 26.1 jit_solution(696700784911240289)
XLA Ops:
  0.0 24.2 %attention_layer.1 = (f32[256,512]{1,0:T(8,128)}, bf16[1,256,512]{2,1,0:T(8,128)(2,1)}) custom-call(s32[16]{0:T(128)} %docs_hbm.1, bf16[256,2048]{1,0:T(8,128)(2,1)} %tok_hbm.1, bf16[2048,1024]{1,0:T(8,128)(2,1)} %wq_hbm.1, bf16[2048,512]{1,0:T(8,128)(2,1)} %wk_hbm.1, bf16[2048,512]{1,0:T(8,128)(2,1)} %wv_hbm.1, bf16[1024,2048]{1,0:T(8,128)(2,1)} %wo_hbm.1, ...), custom_call_target="tpu_custom_call" | custom-call | flops 5100273664 | bytes 10485760 | tf_op jit(solution)/shard_map/attention_layer/pallas_call | solution.py:457
  24.2 1.9 %fusion = bf16[256,512]{1,0:T(8,128)(2,1)} fusion(f32[256,512]{1,0:T(8,128)} %get-tuple-element.7, bf16[1,256,512]{2,1,0:T(8,128)(2,1)} %get-tuple-element.8), kind=kLoop, calls=%fused_computation.1 | loop fusion | flops 393216 | bytes 1048576 | tf_op jit(solution)/shard_map/convert_element_type | solution.py:513

commit v9 on v8

--- a/solution.py
+++ b/solution.py
@@ -148,10 +148,10 @@
     sine = cos_of_turns(turns - 0.25)
     sin2[...] = jnp.where(low, -sine, sine)
 
+    for n in range(q_parts):
+        wq_copy(n).start()
     for copy in first:
         copy.wait()
-    for n in range(q_parts):
-        wq_copy(n).start()
     projected = mm(tok[...], wkv[...])
     kv[0, 0] = norm_rotate(projected[:, :HD], kg[...], cos2[...], sin2[...]).astype(BF16)
     kv[0, 1] = projected[:, HD:].astype(BF16)

time: 26.3 us -> 26.3 us (level)
  no operation moved by 1% of the time
where the time goes in v9:
time: 26.3 us; the launch traced here: 26 us
  Pallas kernels  24.2 us (92%)
  other arithmetic  1.88 us (7%)
    pallas_call x1, Pallas kernels, local(): pl.pallas_call(functools.partial(kernel, reach, n_ctx, n_tp, docs), out_s...  24.2 us
    convert_element_type x1, other arithmetic, local(): return (mine + jnp.sum(others.astype(F32), axis=0)).astype(BF16)  1.88 us

profile of v9, /device:TPU:16, one launch (start us, length us, event | category | flops | bytes accessed | tf_op | source)
XLA Modules:
  0.0 26.0 jit_solution(14034417645499683680)
XLA Ops:
  0.0 24.2 %attention_layer.1 = (f32[256,512]{1,0:T(8,128)}, bf16[1,256,512]{2,1,0:T(8,128)(2,1)}) custom-call(s32[16]{0:T(128)} %docs_hbm.1, bf16[256,2048]{1,0:T(8,128)(2,1)} %tok_hbm.1, bf16[2048,1024]{1,0:T(8,128)(2,1)} %wq_hbm.1, bf16[2048,512]{1,0:T(8,128)(2,1)} %wk_hbm.1, bf16[2048,512]{1,0:T(8,128)(2,1)} %wv_hbm.1, bf16[1024,2048]{1,0:T(8,128)(2,1)} %wo_hbm.1, ...), custom_call_target="tpu_custom_call" | custom-call | flops 5100273664 | bytes 10485760 | tf_op jit(solution)/shard_map/attention_layer/pallas_call | solution.py:457
  24.2 1.9 %fusion = bf16[256,512]{1,0:T(8,128)(2,1)} fusion(f32[256,512]{1,0:T(8,128)} %get-tuple-element.7, bf16[1,256,512]{2,1,0:T(8,128)(2,1)} %get-tuple-element.8), kind=kLoop, calls=%fused_computation.1 | loop fusion | flops 393216 | bytes 1048576 | tf_op jit(solution)/shard_map/convert_element_type | solution.py:513
